TPU v7x, 32 devices: a whole 2x2x4 slice. The times are simulated.
32 devices in a mesh: fsdp: 16 (over z, y, core), mp: 2 (over x).
Axes of the slice: x: 2, y: 2, z: 4, core: 2. Of those that a mesh axis runs over, the one named last changes fastest.
Arguments:
- inputs: bfloat16 [16, 1024, 1024], P('fsdp'), may hold values from -6 to 6
- doc_ids: int32 [16, 1024], P('fsdp'), may hold values from 0 to 3, never falling along the last dimension, each value on 1 to 512 neighbouring positions
- out_grad: bfloat16 [16, 1024, 1024], P('fsdp'), may hold values from -7 to 7
- attn_w: float32 [4, 1024, 1024], P(None, 'fsdp', 'mp'), may hold values from -7 to 7
- attn_mom: float32 [4, 1024, 1024], P(None, 'fsdp', 'mp'), may hold values from -3.2 to 3.2
- attn_avg: float32 [4, 1024, 1024], P(None, 'fsdp', 'mp'), may hold values from -7 to 7
- mlp_w: float32 [3, 1024, 4096], P(None, 'fsdp', 'mp'), may hold values from -7 to 7
- mlp_mom: float32 [3, 1024, 4096], P(None, 'fsdp', 'mp'), may hold values from -3.2 to 3.2
- mlp_avg: float32 [3, 1024, 4096], P(None, 'fsdp', 'mp'), may hold values from -7 to 7
- head_scale: float32 [1024], P('mp'), may hold values from 0.7 to 1.6
- head_mom: float32 [1024], P('mp'), may hold values from -153.6 to 153.6
- mix_rates: float32 [2, 1024], replicated, may hold values from 0.05 to 0.5
- mix_mom: float32 [2, 1024], replicated, may hold values from -512 to 512
- unit_scales: float32 [2, 4096], P(None, 'mp'), may hold values from 0.5 to 2
- unit_mom: float32 [2, 4096], P(None, 'mp'), may hold values from -153.6 to 153.6
Outputs:
- hidden_out: float32 [16, 1024, 1024], P('fsdp')
- input_grad: float32 [16, 1024, 1024], P('fsdp')
- attn_mom_new: float32 [4, 1024, 1024], P(None, 'fsdp', 'mp')
- attn_new: float32 [4, 1024, 1024], P(None, 'fsdp', 'mp')
- attn_avg_new: float32 [4, 1024, 1024], P(None, 'fsdp', 'mp')
- mlp_mom_new: float32 [3, 1024, 4096], P(None, 'fsdp', 'mp')
- mlp_new: float32 [3, 1024, 4096], P(None, 'fsdp', 'mp')
- mlp_avg_new: float32 [3, 1024, 4096], P(None, 'fsdp', 'mp')
- head_mom_new: float32 [1024], P('mp')
- head_new: float32 [1024], P('mp')
- mix_mom_new: float32 [2, 1024], replicated
- mix_new: float32 [2, 1024], replicated
- units_mom_new: float32 [2, 4096], P(None, 'mp')
- units_new: float32 [2, 4096], P(None, 'mp')
Inputs may be any that keep to these rules, and one draw needn't show every extreme that they name: `doc_ids`: along a row the document number never falls; a document spans at most 512 positions.
All inputs are finite; a program needn't handle non-finite values.
Results may differ from a plain program's by a relative error of at most 0.014.
Values may be sent and summed in bfloat16 or wider, within the bound.
A program may use at most 256 MiB of HBM per device.

v0:
```python
import math

import jax
import jax.numpy as jnp
from jax import lax
from jax.sharding import PartitionSpec as P

D = 1024
HD = 64


EPS = 1e-06
MOMENTUM = 0.9
AVERAGE = 0.9
NEG_FILL = -1e30
THETA = 10000.0
RATE_WEIGHT = 50.0
RATE_HEAD = 0.08
RATE_MIX = 0.02
RATE_UNITS = 0.5


def rms_unit(vector):
    return vector * lax.rsqrt(jnp.mean(vector * vector, axis=-1, keepdims=True) + EPS)


def rms_back(vector, grad):
    factor = lax.rsqrt(jnp.mean(vector * vector, axis=-1, keepdims=True) + EPS)
    unit_vec = vector * factor
    return factor * (grad - unit_vec * jnp.mean(grad * unit_vec, axis=-1, keepdims=True))


def rotary_tables(doc_row):
    length = doc_row.shape[0]
    position = jnp.arange(length, dtype=jnp.int32)
    boundary = jnp.concatenate(
        [jnp.ones((1,), jnp.int32), (doc_row[1:] != doc_row[:-1]).astype(jnp.int32)]
    )
    doc_start = lax.cummax(jnp.where(boundary > 0, position, 0), axis=0)
    offset = (position - doc_start).astype(jnp.float32)
    freq = THETA ** (-2.0 * jnp.arange(HD // 2, dtype=jnp.float32) / HD)
    angle = offset[:, None] * freq[None, :]
    return (jnp.cos(angle), jnp.sin(angle))


def rotate(vector, cos_table, sin_table):
    half_dim = vector.shape[-1] // 2
    lower_half = vector[..., :half_dim]
    upper_half = vector[..., half_dim:]
    cos_part = cos_table[:, None, :]
    sin_part = sin_table[:, None, :]
    return jnp.concatenate(
        [
            lower_half * cos_part - upper_half * sin_part,
            lower_half * sin_part + upper_half * cos_part,
        ],
        axis=-1,
    )


def rotate_back(grad, cos_table, sin_table):
    half_dim = grad.shape[-1] // 2
    lower_half = grad[..., :half_dim]
    upper_half = grad[..., half_dim:]
    cos_part = cos_table[:, None, :]
    sin_part = sin_table[:, None, :]
    return jnp.concatenate(
        [
            lower_half * cos_part + upper_half * sin_part,
            upper_half * cos_part - lower_half * sin_part,
        ],
        axis=-1,
    )


def nesterov(param, moment, grad, step_rate):
    moment_new = MOMENTUM * moment + grad
    return (moment_new, param - step_rate * (grad + MOMENTUM * moment_new))


def local(
    inputs,
    doc_ids,
    out_grad,
    attn_w,
    attn_mom,
    attn_avg,
    mlp_w,
    mlp_mom,
    mlp_avg,
    head_scale,
    head_mom,
    mix_rates,
    mix_mom,
    unit_scales,
    unit_mom,
):
    length = inputs.shape[1]
    model_width = inputs.shape[2]
    head_count = head_scale.shape[0] // HD
    block_rows = min(512, length)
    block_count = length // block_rows
    tokens = inputs.shape[0] * lax.axis_size("fsdp") * length
    doc_row = doc_ids[0]
    input_low = inputs[0]
    resid_in = input_low.astype(jnp.float32)
    cos_table, sin_table = rotary_tables(doc_row)
    position = jnp.arange(length, dtype=jnp.int32)
    attn_full = lax.all_gather(attn_w.astype(jnp.bfloat16), "fsdp", axis=1, tiled=True)
    projected = jnp.einsum(
        "sd,jdc->jsc", input_low, attn_full[:3], preferred_element_type=jnp.float32
    )
    head_gain = head_scale.reshape(head_count, HD)
    q_rot = rotate(projected[0].reshape(length, head_count, HD), cos_table, sin_table)
    k_rot = rotate(projected[1].reshape(length, head_count, HD), cos_table, sin_table)
    q_unit = rms_unit(q_rot)
    k_unit = rms_unit(k_rot)
    query_low = (head_gain * q_unit).astype(jnp.bfloat16)
    key_low = (head_gain * k_unit).astype(jnp.bfloat16)
    value_low = projected[2].reshape(length, head_count, HD).astype(jnp.bfloat16)

    def scores_of(row_first):
        query_blk = lax.dynamic_slice_in_dim(query_low, row_first, block_rows, 0)
        raw_scores = jnp.einsum(
            "qhe,khe->hqk", query_blk, key_low, preferred_element_type=jnp.float32
        )
        row_pos = lax.dynamic_slice_in_dim(position, row_first, block_rows, 0)
        row_docs = lax.dynamic_slice_in_dim(doc_row, row_first, block_rows, 0)
        allowed = (row_docs[:, None] == doc_row[None, :]) & (position[None, :] <= row_pos[:, None])
        return (jnp.where(allowed[None], raw_scores * HD ** (-0.5), NEG_FILL), query_blk)

    def attend(accums, blk_index):
        scores, query_blk = scores_of(blk_index * block_rows)
        peak_val = jnp.max(scores, axis=-1, keepdims=True)
        expo_vals = jnp.exp(scores - peak_val)
        row_total = jnp.sum(expo_vals, axis=-1, keepdims=True)
        probs_low = (expo_vals / row_total).astype(jnp.bfloat16)
        blk_out = jnp.einsum(
            "hqk,khe->qhe", probs_low, value_low, preferred_element_type=jnp.float32
        )
        return (accums, (blk_out, (peak_val + jnp.log(row_total))[..., 0]))

    _, (mixed_blocks, log_totals) = lax.scan(attend, None, jnp.arange(block_count))
    mixed_low = mixed_blocks.reshape(length, head_count * HD).astype(jnp.bfloat16)
    attn_part = jnp.einsum("sc,dc->sd", mixed_low, attn_full[3], preferred_element_type=jnp.float32)
    attn_out = lax.psum(attn_part, "mp")
    attn_unit = rms_unit(attn_out)
    resid_one = resid_in + mix_rates[0] * (attn_unit - resid_in)
    hidden_one = rms_unit(resid_one)
    hidden_low = hidden_one.astype(jnp.bfloat16)
    mlp_full = lax.all_gather(mlp_w.astype(jnp.bfloat16), "fsdp", axis=1, tiled=True)
    gates = jnp.einsum("sd,jdf->jsf", hidden_low, mlp_full[:2], preferred_element_type=jnp.float32)
    up_proj = gates[0]
    gate_proj = gates[1]
    gate_arg = unit_scales[1] * gate_proj * D ** (-0.5)
    gate_sig = jax.nn.sigmoid(gate_arg)
    gate_act = gate_arg * gate_sig
    units_low = (unit_scales[0] * up_proj * gate_act).astype(jnp.bfloat16)
    mlp_part = jnp.einsum("sf,df->sd", units_low, mlp_full[2], preferred_element_type=jnp.float32)
    mlp_out = lax.psum(mlp_part, "mp")
    mlp_unit = rms_unit(mlp_out)
    resid_two = hidden_one + mix_rates[1] * (mlp_unit - hidden_one)
    result = rms_unit(resid_two)
    cotangent = out_grad[0].astype(jnp.float32)
    d_resid_two = rms_back(resid_two, cotangent)
    grad_mix_mlp = jnp.sum(d_resid_two * (mlp_unit - hidden_one), axis=0)
    d_hidden_one = d_resid_two * (1.0 - mix_rates[1])
    d_mlp_low = rms_back(mlp_out, mix_rates[1] * d_resid_two).astype(jnp.bfloat16)
    mlp_back = lax.all_gather(mlp_w.astype(jnp.bfloat16), "fsdp", axis=1, tiled=True)
    d_units = jnp.einsum("sd,df->sf", d_mlp_low, mlp_back[2], preferred_element_type=jnp.float32)
    d_up = d_units * unit_scales[0] * gate_act
    d_arg = d_units * unit_scales[0] * up_proj * gate_sig * (1.0 + gate_arg * (1.0 - gate_sig))
    d_gate = d_arg * unit_scales[1] * D ** (-0.5)
    grad_units = jnp.stack(
        [
            jnp.sum(d_units * up_proj * gate_act, axis=0),
            jnp.sum(d_arg * gate_proj * D ** (-0.5), axis=0),
        ]
    )
    d_gates_low = jnp.stack([d_up, d_gate]).astype(jnp.bfloat16)
    mlp_back_part = jnp.einsum(
        "jsf,jdf->sd", d_gates_low, mlp_back[:2], preferred_element_type=jnp.float32
    )
    d_hidden_one = d_hidden_one + lax.psum(mlp_back_part, "mp")
    right_cols = d_mlp_low
    left_cols = hidden_low
    grad_mlp = jnp.transpose(
        lax.psum_scatter(
            jnp.concatenate(
                [
                    jnp.einsum(
                        "sd,jsf->djf", left_cols, d_gates_low, preferred_element_type=jnp.float32
                    ),
                    jnp.einsum(
                        "sd,sf->df", right_cols, units_low, preferred_element_type=jnp.float32
                    )[:, None, :],
                ],
                axis=1,
            ),
            "fsdp",
            scatter_dimension=0,
            tiled=True,
        ),
        (1, 0, 2),
    )
    d_resid_one = rms_back(resid_one, d_hidden_one)
    grad_mix_attn = jnp.sum(d_resid_one * (attn_unit - resid_in), axis=0)
    d_resid_in = d_resid_one * (1.0 - mix_rates[0])
    d_attn_low = rms_back(attn_out, mix_rates[0] * d_resid_one).astype(jnp.bfloat16)
    attn_back = lax.all_gather(attn_w.astype(jnp.bfloat16), "fsdp", axis=1, tiled=True)
    d_mixed = jnp.einsum("sd,dc->sc", d_attn_low, attn_back[3], preferred_element_type=jnp.float32)
    d_mixed = d_mixed.astype(jnp.bfloat16).reshape(length, head_count, HD)

    def attend_back(accums, blk_index):
        d_key, d_value = accums
        row_first = blk_index * block_rows
        scores, query_blk = scores_of(row_first)
        blk_total = lax.dynamic_index_in_dim(log_totals, blk_index, 0, keepdims=False)
        attn_probs = jnp.exp(scores - blk_total[..., None])
        d_out_blk = lax.dynamic_slice_in_dim(d_mixed, row_first, block_rows, 0)
        d_probs = jnp.einsum(
            "qhe,khe->hqk", d_out_blk, value_low, preferred_element_type=jnp.float32
        )
        d_scores = attn_probs * (d_probs - jnp.sum(attn_probs * d_probs, axis=-1, keepdims=True))
        d_raw_low = (d_scores * HD ** (-0.5)).astype(jnp.bfloat16)
        d_query = jnp.einsum("hqk,khe->qhe", d_raw_low, key_low, preferred_element_type=jnp.float32)
        d_key = d_key + jnp.einsum(
            "hqk,qhe->khe", d_raw_low, query_blk, preferred_element_type=jnp.float32
        )
        d_value = d_value + jnp.einsum(
            "hqk,qhe->khe",
            attn_probs.astype(jnp.bfloat16),
            d_out_blk,
            preferred_element_type=jnp.float32,
        )
        return ((d_key, d_value), d_query)

    zero_heads = jnp.zeros((length, head_count, HD), jnp.float32)
    (d_key_all, d_value_all), d_query_blocks = lax.scan(
        attend_back, (zero_heads, zero_heads), jnp.arange(block_count)
    )
    d_query_all = d_query_blocks.reshape(length, head_count, HD)
    grad_head = jnp.sum(d_query_all * q_unit + d_key_all * k_unit, axis=0).reshape(-1)
    d_query_raw = rotate_back(rms_back(q_rot, head_gain * d_query_all), cos_table, sin_table)
    d_key_raw = rotate_back(rms_back(k_rot, head_gain * d_key_all), cos_table, sin_table)
    d_proj_low = jnp.stack(
        [
            d_query_raw.reshape(length, -1),
            d_key_raw.reshape(length, -1),
            d_value_all.reshape(length, -1),
        ]
    ).astype(jnp.bfloat16)
    grad_mix = jnp.stack([grad_mix_attn, grad_mix_mlp])
    grad_head, grad_mix, grad_units = lax.psum((grad_head, grad_mix, grad_units), "fsdp")
    attn_back_part = jnp.einsum(
        "jsc,jdc->sd", d_proj_low, attn_back[:3], preferred_element_type=jnp.float32
    )
    input_grad = d_resid_in + lax.psum(attn_back_part.astype(jnp.bfloat16), "mp").astype(
        jnp.float32
    )
    left_cols = input_low
    right_cols = d_attn_low
    in_terms = jnp.einsum("sd,jsc->djc", left_cols, d_proj_low, preferred_element_type=jnp.float32)
    out_terms = jnp.einsum("sd,sc->dc", right_cols, mixed_low, preferred_element_type=jnp.float32)
    grad_attn = jnp.transpose(
        lax.psum_scatter(
            jnp.concatenate([in_terms, out_terms[:, None, :]], axis=1),
            "fsdp",
            scatter_dimension=0,
            tiled=True,
        ),
        (1, 0, 2),
    )
    root_tokens = math.sqrt(tokens)
    weight_rate = RATE_WEIGHT / root_tokens
    attn_mom_new, attn_step = nesterov(attn_w, attn_mom, grad_attn, weight_rate)
    mlp_mom_new, mlp_step = nesterov(mlp_w, mlp_mom, grad_mlp, weight_rate)
    attn_squares = jnp.sum(attn_step * attn_step, axis=1)
    mlp_squares = jnp.sum(mlp_step * mlp_step, axis=1)
    attn_squares, mlp_squares = lax.psum((attn_squares, mlp_squares), "fsdp")
    attn_new = attn_step * lax.rsqrt(attn_squares[:, None, :] / model_width + EPS)
    mlp_new = mlp_step * lax.rsqrt(mlp_squares[:, None, :] / model_width + EPS)
    head_mom_new, head_new = nesterov(head_scale, head_mom, grad_head, RATE_HEAD / root_tokens)
    mix_mom_new, mix_new = nesterov(mix_rates, mix_mom, grad_mix, RATE_MIX / root_tokens)
    units_mom_new, units_new = nesterov(unit_scales, unit_mom, grad_units, RATE_UNITS / root_tokens)
    return (
        result[None],
        input_grad[None],
        attn_mom_new,
        attn_new,
        AVERAGE * attn_avg + (1.0 - AVERAGE) * attn_new,
        mlp_mom_new,
        mlp_new,
        AVERAGE * mlp_avg + (1.0 - AVERAGE) * mlp_new,
        head_mom_new,
        head_new,
        mix_mom_new,
        mix_new,
        units_mom_new,
        units_new,
    )


def solution(mesh):
    placed = (
        P("fsdp", None, None),
        P("fsdp", None),
        P("fsdp", None, None),
        P(None, "fsdp", "mp"),
        P(None, "fsdp", "mp"),
        P(None, "fsdp", "mp"),
        P(None, "fsdp", "mp"),
        P(None, "fsdp", "mp"),
        P(None, "fsdp", "mp"),
        P("mp"),
        P("mp"),
        P(),
        P(),
        P(None, "mp"),
        P(None, "mp"),
    )
    return jax.shard_map(
        local,
        mesh=mesh,
        in_specs=placed,
        out_specs=(
            P("fsdp", None, None),
            P("fsdp", None, None),
            P(None, "fsdp", "mp"),
            P(None, "fsdp", "mp"),
            P(None, "fsdp", "mp"),
            P(None, "fsdp", "mp"),
            P(None, "fsdp", "mp"),
            P(None, "fsdp", "mp"),
            P("mp"),
            P("mp"),
            P(),
            P(),
            P(None, "mp"),
            P(None, "mp"),
        ),
        check_vma=False,
    )
```

profile of v0, /device:TPU:0, one launch (start us, length us, event | category | flops | bytes accessed | tf_op | source)
XLA Modules:
  0.0 1432.0 jit_solution(1757144328400162072)
XLA Ops:
  12.4 51.6 %all-gather.3.cloned.1.call-done = bf16[4,1024,512]{2,0,1:T(4,128)(2,1)} async-done(((bf16[4,64,512]{2,0,1:T(4,128)(2,1)}), bf16[4,1024,512]{2,0,1:T(4,128)(2,1)}) %all-gather.3.cloned.1.call-update) | async-done | bytes 4194320 | tf_op jit(solution)/shard_map/all_gather | solution.py:109
  80.7 31.5 %while.29 = (s32[]{:T(128)}, bf16[2,512,8,64]{1,3,2,0:T(8,128)(2,1)S(1)}, f32[2,8,512]{2,1,0:T(8,128)S(1)}, s32[2]{0:T(128)S(1)}, s32[1024]{0:T(1024)S(1)}, /*in...) while((s32[]{:T(128)}, ...), condition=%wide.region_7.8_spmd.clone, body=%wide.region_4.7_spmd.clone.sunk | while | flops 1125642240 | bytes 56250584 | solution.py:143
  125.1 103.4 %all-reduce.8.cloned.1.call-done = f32[1024,1024]{1,0:T(8,128)} async-done(((f32[1024,1024]{1,0:T(8,128)}), f32[1024,1024]{1,0:T(8,128)}) %all-reduce.8.cloned.1.call-update) | async-done | bytes 4194320 | tf_op jit(solution)/shard_map/psum | solution.py:146
  237.0 95.4 %all-gather.5.cloned.1.call-done = bf16[3,1024,2048]{2,1,0:T(8,128)(2,1)} async-done(((bf16[3,64,2048]{2,1,0:T(8,128)(2,1)}), bf16[3,1024,2048]{2,1,0:T(8,128)(2,1)}) %all-gather.5.cloned.1.call-update) | async-done | bytes 12582928 | tf_op jit(solution)/shard_map/all_gather | solution.py:151
  332.4 13.0 fusion.58
  351.2 9.6 fusion.67
  360.8 106.1 %all-reduce.10.cloned.1.call-done = f32[1024,1024]{1,0:T(8,128)} async-done(((f32[1024,1024]{1,0:T(8,128)}), f32[1024,1024]{1,0:T(8,128)}) %all-reduce.10.cloned.1.call-update) | async-done | bytes 4194320 | tf_op jit(solution)/shard_map/psum | solution.py:160
  479.4 18.0 %fusion.49 = (f32[2048]{0:T(1024)}, f32[2048]{0:T(1024)}, f32[1024,2048]{1,0:T(8,128)}, bf16[1,1024,2048]{2,1,0:T(8,128)(2,1)S(1)}) fusion(f32[2,1024,2048]{2,1,0:T(8,128)} %copy-done.95, f32[2048]{0:T(1024)S(1)} %bitcast.275, f32[2048]{0:T(1024)S(1)} %bitcast.282, bf16[3,1024,2048]{2,1,0:T(8,128)(2,1)} %all-gather.5.cloned.1.call-done, ...), kind=kOutput, calls=%fused_computation.55 | convolution fusion | flops 4354732032 | bytes 44097536 | tf_op jit(solution)/shard_map/sd,df->sf/dot_general | solution.py:170
  505.4 12.6 fusion.71
  524.8 101.2 %all-reduce.12.cloned.1.call-done = f32[1024,1024]{1,0:T(8,128)} async-done(((f32[1024,1024]{1,0:T(8,128)}), f32[1024,1024]{1,0:T(8,128)}) %all-reduce.12.cloned.1.call-update) | async-done | bytes 4194320 | tf_op jit(solution)/shard_map/psum | solution.py:184
  648.2 193.3 %while.30 = (s32[]{:T(128)}, f32[1024,8,64]{0,2,1:T(8,128)}, f32[1024,8,64]{0,2,1:T(8,128)}, f32[2,512,8,64]{1,0,3,2:T(2,128)}, s32[2]{0:T(128)S(1)}, /*index=5*...) while((s32[]{:T(128)}, f32[1024,8,64]{0,2,1:T(8,128)}, ...), condition=%wide.region_21.22_spmd.clone.clone, body=%wide.region_19.21_spmd.clone.clone.sunk | while | flops 2746755072 | bytes 238096720 | solution.py:239
  673.8 25.4 %fusion.146 = f32[1,512,8,64]{1,3,2,0:T(8,128)} fusion(bf16[1024,8,64]{0,2,1:T(8,128)(2,1)S(1)} %get-tuple-element.639, f32[8,512,1024]{2,1,0:T(8,128)} %copy-done, f32[8,512,1024]{2,1,0:T(8,128)} %fusion.145), kind=kOutput, calls=%fused_computation.29.clone.1 | convolution fusion | flops 557847552 | bytes 35651584 | tf_op jit(solution)/shard_map/while/body/eval_jaxpr/hqk,khe->qhe/dot_general | solution.py:226
  699.3 23.3 %bitcast_add_fusion.7 = f32[1024,8,64]{0,2,1:T(8,128)} fusion(f32[1024,8,64]{0,2,1:T(8,128)} %get-tuple-element.613, f32[8,512,1024]{2,1,0:T(8,128)} %copy-done, f32[8,512,1024]{2,1,0:T(8,128)} %fusion.145, pred[]{:T(512)S(6)} %compare.3, bf16[1024,8,64]{0,2,1:T(8,128)(2,1)} %get-tuple-element.635, s32[]{:T(128)S(6)} %select_n.65), kind=kOutput, calls=%fused_computation.27.clone.1 | convolution fusion | flops 558896128 | bytes 71827464 | tf_op jit(solution)/shard_map/while/body/eval_jaxpr/hqk,qhe->khe/dot_general | solution.py:227
  724.9 19.6 %dynamic_update_slice.22 = f32[2,512,8,64]{1,0,3,2:T(2,128)} dynamic-update-slice(f32[2,512,8,64]{1,0,3,2:T(2,128)} %get-tuple-element.615, f32[1,512,8,64]{1,0,3,2:T(1,128)S(1)} %copy.147, s32[]{:T(128)S(6)} %copy.167, s32[]{:T(128)} %constant.37.clone.1..sunk.1, s32[]{:T(128)} %constant.37.clone.1..sunk.1, s32[]{:T(128)} %constant.37.clone.1..sunk.1) | dynamic-update-slice | bytes 2097156 | tf_op jit(solution)/shard_map/while/body/jit(dynamic_update_index_in_dim)/dynamic_update_slice | solution.py:143
  770.3 25.4 %fusion.146 = f32[1,512,8,64]{1,3,2,0:T(8,128)} fusion(bf16[1024,8,64]{0,2,1:T(8,128)(2,1)S(1)} %get-tuple-element.639, f32[8,512,1024]{2,1,0:T(8,128)} %copy-done, f32[8,512,1024]{2,1,0:T(8,128)} %fusion.145), kind=kOutput, calls=%fused_computation.29.clone.1 | convolution fusion | flops 557847552 | bytes 35651584 | tf_op jit(solution)/shard_map/while/body/eval_jaxpr/hqk,khe->qhe/dot_general | solution.py:226
  795.7 24.0 %bitcast_add_fusion.7 = f32[1024,8,64]{0,2,1:T(8,128)} fusion(f32[1024,8,64]{0,2,1:T(8,128)} %get-tuple-element.613, f32[8,512,1024]{2,1,0:T(8,128)} %copy-done, f32[8,512,1024]{2,1,0:T(8,128)} %fusion.145, pred[]{:T(512)S(6)} %compare.3, bf16[1024,8,64]{0,2,1:T(8,128)(2,1)} %get-tuple-element.635, s32[]{:T(128)S(6)} %select_n.65), kind=kOutput, calls=%fused_computation.27.clone.1 | convolution fusion | flops 558896128 | bytes 71827464 | tf_op jit(solution)/shard_map/while/body/eval_jaxpr/hqk,qhe->khe/dot_general | solution.py:227
  822.0 19.6 %dynamic_update_slice.22 = f32[2,512,8,64]{1,0,3,2:T(2,128)} dynamic-update-slice(f32[2,512,8,64]{1,0,3,2:T(2,128)} %get-tuple-element.615, f32[1,512,8,64]{1,0,3,2:T(1,128)S(1)} %copy.147, s32[]{:T(128)S(6)} %copy.167, s32[]{:T(128)} %constant.37.clone.1..sunk.1, s32[]{:T(128)} %constant.37.clone.1..sunk.1, s32[]{:T(128)} %constant.37.clone.1..sunk.1) | dynamic-update-slice | bytes 2097156 | tf_op jit(solution)/shard_map/while/body/jit(dynamic_update_index_in_dim)/dynamic_update_slice | solution.py:143
  878.2 10.2 copy.95
  889.1 17.6 %fusion.61 = f32[1024,2,2048]{2,0,1:T(8,128)} fusion(bf16[1,1024,2048]{2,1,0:T(8,128)(2,1)} %copy-done.35, bf16[1,1024,2048]{2,1,0:T(8,128)(2,1)} %copy-done.94, f32[1024,1024]{1,0:T(8,128)} %get-tuple-element.376, f32[1024]{0:T(1024)S(1)} %copy-done.62), kind=kOutput, calls=%fused_computation.71 | convolution fusion | flops 8608808960 | bytes 29364224 | tf_op jit(solution)/shard_map/sd,jsf->djf/dot_general | solution.py:191
  906.7 16.5 %convolution_bitcast_fusion = f32[1024,1,2048]{2,0,1:T(8,128)} fusion(f32[2,1024,2048]{2,1,0:T(8,128)} %copy-done.95, f32[2048]{0:T(1024)S(1)} %bitcast.283, f32[2048]{0:T(1024)S(1)} %bitcast.277, f32[1024,1024]{1,0:T(8,128)S(1)} %copy-done.6, bf16[1,1024,1024]{2,1,0:T(8,128)(2,1)S(1)} %copy-done.15, f32[1024]{0:T(1024)S(1)} %copy-done.91, ...), kind=kOutput, calls=%fused_computation.76 | convolution fusion | flops 4329570304 | bytes 35692544 | tf_op jit(solution)/shard_map/sd,sf->df/dot_general | solution.py:194
  923.3 18.7 %pad_maximum_fusion = f32[1024,3,2048]{2,0,1:T(8,128)} fusion(f32[1024,1,2048]{2,0,1:T(8,128)} %convolution_bitcast_fusion, f32[1024,2,2048]{2,0,1:T(8,128)} %fusion.61), kind=kLoop, calls=%fused_computation.44 | loop fusion | flops 6291456 | bytes 50331648 | tf_op jit(solution)/shard_map/concatenate | solution.py:189
  950.2 153.9 %all-reduce.16.cloned.1.call-done = f32[1024,4,512]{2,1,0:T(4,128)} async-done(((f32[1024,4,512]{2,1,0:T(4,128)}), f32[1024,4,512]{2,1,0:T(4,128)}) %all-reduce.16.cloned.1.call-update) | async-done | bytes 8388624
  1107.8 244.8 %reduce-scatter.2.cloned.1.call-done = f32[64,3,2048]{2,0,1:T(8,128)} async-done(((f32[1024,3,2048]{2,0,1:T(8,128)}), f32[64,3,2048]{2,0,1:T(8,128)}) %reduce-scatter.2.cloned.1.call-update) | async-done | bytes 1572880 | tf_op jit(solution)/shard_map/reduce_scatter | solution.py:188
  1356.3 60.4 %all-reduce.1 = (f32[4,512]{1,0:T(4,128)S(1)}, f32[3,2048]{1,0:T(4,128)S(1)}, f32[512]{0:T(512)S(1)}, f32[2,1024]{1,0:T(2,128)S(1)}, f32[2,2048]{1,0:T(2,128)S(1)}) all-reduce(f32[4,512]{1,0:T(4,128)S(1)} %get-tuple-element.371, f32[3,2048]{1,0:T(4,128)S(1)} %get-tuple-element.369, ...), channel_id=1, replica_groups=mesh['fsdp'=16,'mp'=2] {'fsdp'}, use_global_device_ids=true, to_apply=%region_27.28 | all-reduce | flops 14848 | bytes 118784 | tf_op jit(solution)/shard_map/psum | solution.py:280
  (338 shorter events, 238.0 us)
Async XLA Ops:
  7.2 56.9 %all-gather.3.cloned.1.call-start = ((), (), s32[]{:S(2)}) async-start(), calls=%async_computation.1 | async-start | bytes 4456448 | tf_op jit(solution)/shard_map/all_gather | solution.py:109
  9.5 219.1 %all-reduce.8.cloned.1.call-start = ((), (), s32[]{:S(2)}) async-start(), calls=%async_computation.2 | async-start | bytes 8388608 | tf_op jit(solution)/shard_map/psum | solution.py:146
  122.0 210.3 %all-gather.5.cloned.1.call-start = ((), (), s32[]{:S(2)}) async-start(), calls=%async_computation.3 | async-start | bytes 13369344 | tf_op jit(solution)/shard_map/all_gather | solution.py:151
  124.4 342.5 %all-reduce.10.cloned.1.call-start = ((), (), s32[]{:S(2)}) async-start(), calls=%async_computation.4 | async-start | bytes 8388608 | tf_op jit(solution)/shard_map/psum | solution.py:160
  125.1 507.9 %copy-start.65 = (f32[1,1024]{1,0:T(1,128)}, f32[1,1024]{1,0:T(1,128)S(1)}, u32[]{:S(2)}) copy-start(f32[1,1024]{1,0:T(1,128)S(1)} %get-tuple-element.401) | copy-start | bytes 12292
  125.1 354.2 %copy-start.86 = (f32[1,2048]{1,0:T(1,128)}, f32[1,2048]{1,0:T(1,128)S(1)}, u32[]{:S(2)}) copy-start(f32[1,2048]{1,0:T(1,128)S(1)} %get-tuple-element.396) | copy-start | bytes 24580
  125.1 372.2 %copy-start.78 = (f32[1,2048]{1,0:T(1,128)}, f32[1,2048]{1,0:T(1,128)S(1)}, u32[]{:S(2)}) copy-start(f32[1,2048]{1,0:T(1,128)S(1)} %get-tuple-element.397) | copy-start | bytes 24580
  237.0 396.0 %copy-start.61 = (f32[1024]{0:T(1024)}, f32[1024]{0:T(1024)S(1)}, u32[]{:S(2)}) copy-start(f32[1024]{0:T(1024)S(1)} %add_rsqrt_fusion.6) | copy-start | bytes 12292
  360.8 265.2 %all-reduce.12.cloned.1.call-start = ((), (), s32[]{:S(2)}) async-start(), calls=%async_computation.5 | async-start | bytes 8388608 | tf_op jit(solution)/shard_map/psum | solution.py:184
  469.7 163.3 %copy-start.63 = (f32[1024]{0:T(1024)}, f32[1024]{0:T(1024)S(1)}, u32[]{:S(2)}) copy-start(f32[1024]{0:T(1024)S(1)} %add_rsqrt_fusion.5) | copy-start | bytes 12292
  474.6 158.5 %copy-start.68 = (f32[1024]{0:T(1024)}, f32[1024]{0:T(1024)S(1)}, u32[]{:S(2)}) copy-start(f32[1024]{0:T(1024)S(1)} %add_rsqrt_fusion.4) | copy-start | bytes 12292
  476.6 156.4 %copy-start.72 = (f32[1024]{0:T(1024)}, f32[1024]{0:T(1024)S(1)}, u32[]{:S(2)}) copy-start(f32[1024]{0:T(1024)S(1)} %broadcast_multiply_fusion.6) | copy-start | bytes 12292
  518.0 426.0 %all-reduce.14.cloned.1.call-start = ((), (), s32[]{:S(2)}) async-start(), calls=%async_computation.6 | async-start | bytes 4194304 | tf_op jit(solution)/shard_map/psum | solution.py:258
  867.3 236.8 %all-reduce.16.cloned.1.call-start = ((), (), s32[]{:S(2)}) async-start(), calls=%async_computation.8 | async-start | bytes 16777216
  888.5 464.1 %reduce-scatter.2.cloned.1.call-start = ((), (), s32[]{:S(2)}) async-start(), calls=%async_computation.7 | async-start | bytes 26738688 | tf_op jit(solution)/shard_map/reduce_scatter | solution.py:188
  944.1 160.1 %copy-start.38 = (f32[4,64,512]{2,1,0:T(8,128)S(1)}, f32[4,64,512]{2,1,0:T(8,128)}, u32[]{:S(2)}) copy-start(f32[4,64,512]{2,1,0:T(8,128)} %param.22) | copy-start | bytes 1572868
  944.1 160.1 %copy-start.58 = (f32[4,64,512]{2,1,0:T(8,128)S(1)}, f32[4,64,512]{2,1,0:T(8,128)}, u32[]{:S(2)}) copy-start(f32[4,64,512]{2,1,0:T(8,128)} %param.23) | copy-start | bytes 1572868
  950.2 402.4 %copy-start.26 = (f32[3,64,2048]{2,1,0:T(8,128)S(1)}, f32[3,64,2048]{2,1,0:T(8,128)}, u32[]{:S(2)}) copy-start(f32[3,64,2048]{2,1,0:T(8,128)} %param.25) | copy-start | bytes 4718596
  1107.8 312.7 %copy-start.85 = (f32[512]{0:T(512)S(1)}, f32[512]{0:T(512)}, u32[]{:S(2)}) copy-start(f32[512]{0:T(512)} %param.28) | copy-start | bytes 6148
  1107.8 312.7 %copy-start.92 = (f32[512]{0:T(512)S(1)}, f32[512]{0:T(512)}, u32[]{:S(2)}) copy-start(f32[512]{0:T(512)} %param.29) | copy-start | bytes 6148
  1107.8 313.3 %copy-start.77 = (f32[2,1024]{1,0:T(2,128)S(1)}, f32[2,1024]{1,0:T(2,128)}, u32[]{:S(2)}) copy-start(f32[2,1024]{1,0:T(2,128)} %param.30) | copy-start | bytes 24580
  1107.8 313.3 %copy-start.84 = (f32[2,1024]{1,0:T(2,128)S(1)}, f32[2,1024]{1,0:T(2,128)}, u32[]{:S(2)}) copy-start(f32[2,1024]{1,0:T(2,128)} %param.31) | copy-start | bytes 24580
  1107.8 313.9 %copy-start.75 = (f32[2,2048]{1,0:T(2,128)S(1)}, f32[2,2048]{1,0:T(2,128)}, u32[]{:S(2)}) copy-start(f32[2,2048]{1,0:T(2,128)} %param.32) | copy-start | bytes 49156
  1107.8 313.9 %copy-start.83 = (f32[2,2048]{1,0:T(2,128)S(1)}, f32[2,2048]{1,0:T(2,128)}, u32[]{:S(2)}) copy-start(f32[2,2048]{1,0:T(2,128)} %param.33) | copy-start | bytes 49156
  (81 other events, 790.2 us)
Sparse Core Ops, SparseCore 0:
  10.8 53.2 all-gather.2
  122.2 106.3 all-reduce.7
  231.6 100.7 all-gather.4
  360.9 106.0 all-reduce.9
  518.1 107.8 all-reduce.11
  867.5 62.9 all-reduce.13
  934.2 169.9 all-reduce.15
  1108.8 243.7 reduce-scatter.1
where the time goes:
time: 1450 us; the launch traced here: 1430 us
  waiting for transfers between devices  857 us (59%)
  matrix products  271 us (19%)
  local copies, waits for them, and re-layouts  111 us (8%)
  other arithmetic  109 us (8%)
  blocking collectives  60.4 us (4%)
  between operations  16.4 us (1%)
    reduce_scatter x1, waiting for transfers between devices, local(): lax.psum_scatter(jnp.concatenate([jnp.einsum('sd,jsf->djf', left_cols, d_...  245 us
    unnamed x9, waiting for transfers between devices  154 us
    psum x1, waiting for transfers between devices, local(): mlp_out = lax.psum(mlp_part, 'mp')  106 us
    psum x1, waiting for transfers between devices, local(): attn_out = lax.psum(attn_part, 'mp')  103 us
    psum x1, waiting for transfers between devices, local(): d_hidden_one = d_hidden_one + lax.psum(mlp_back_part, 'mp')  101 us
    all_gather x1, waiting for transfers between devices, local(): lax.all_gather(mlp_w.astype(jnp.bfloat16), 'fsdp', axis=1, tiled=True)  95.4 us
    psum x1, blocking collectives, local(): attn_squares, mlp_squares = lax.psum((attn_squares, mlp_squares), 'fsdp')  60.4 us
    all_gather x1, waiting for transfers between devices, local(): lax.all_gather(attn_w.astype(jnp.bfloat16), 'fsdp', axis=1, tiled=True)  51.6 us
  transfers between devices with their start and end apart: 8, of which 7 were waited for; matrix products, arithmetic and copies ran while one was open for 7% of the time, Pallas kernels for 0%

commit v1 on v0

--- a/solution.py
+++ b/solution.py
@@ -1,8 +1,11 @@
+import functools
 import math
 
 import jax
 import jax.numpy as jnp
 from jax import lax
+from jax.experimental import pallas as pl
+from jax.experimental.pallas import tpu as pltpu
 from jax.sharding import PartitionSpec as P
 
 D = 1024
@@ -76,6 +79,404 @@
 def nesterov(param, moment, grad, step_rate):
     moment_new = MOMENTUM * moment + grad
     return (moment_new, param - step_rate * (grad + MOMENTUM * moment_new))
+
+
+BF = jnp.bfloat16
+F32 = jnp.float32
+MESH = pl.DeviceIdType.MESH
+VM = pltpu.VMEM
+MIB = 1 << 20
+
+
+def dot_nn(a, b):
+    return lax.dot_general(a, b, (((1,), (0,)), ((), ())), preferred_element_type=F32)
+
+
+def dot_nt(a, b):
+    return lax.dot_general(a, b, (((1,), (1,)), ((), ())), preferred_element_type=F32)
+
+
+def dot_tn(a, b):
+    return lax.dot_general(a, b, (((0,), (0,)), ((), ())), preferred_element_type=F32)
+
+
+def split_dot(a, ones):
+    high = a.astype(BF)
+    return dot_nn(high, ones) + dot_nn((a - high.astype(F32)).astype(BF), ones)
+
+
+def ring_place(index, chips):
+    z, y = index // 4, (index // 2) % 2
+    return z + y * (chips - 1 - 2 * z), index % 2
+
+
+def ring_device(place, core, chips):
+    y = place // (chips // 2)
+    return ((place + y * (chips - 1 - 2 * place)) * 2 + y) * 2 + core
+
+
+def greet(peers):
+    barrier = pltpu.get_barrier_semaphore()
+    for peer in peers:
+        pl.semaphore_signal(barrier, inc=1, device_id=peer, device_id_type=MESH)
+    pl.semaphore_wait(barrier, len(peers))
+
+
+def remote(src, dst, send, recv, peer):
+    return pltpu.make_async_remote_copy(
+        src_ref=src, dst_ref=dst, send_sem=send, recv_sem=recv, device_id=peer, device_id_type=MESH
+    )
+
+
+GATHER_GROUPS = ((0, 0, 3), (0, 3, 1), (1, 0, 1), (1, 1, 1), (1, 2, 1))
+
+
+def hops(group, chips):
+    long, short = chips // 2, chips - 1 - chips // 2
+    return (long, short) if group % 2 == 0 else (short, long)
+
+
+def gather_kernel(
+    chips, attn_ref, mlp_ref, attn_out, mlp_out, wo_out,
+    ring_send, ring_recv, pair_send, pair_recv, own_sem, wo_send, wo_recv,
+):
+    index, x = lax.axis_index("fsdp"), lax.axis_index("mp")
+    place, core = ring_place(index, chips)
+    rows = attn_ref.shape[1]
+    right = (ring_device((place + 1) % chips, core, chips), x)
+    left = (ring_device((place + chips - 1) % chips, core, chips), x)
+    pair = (index + 1 - 2 * core, x)
+    across = (index, 1 - x)
+    greet((right, left, pair, across))
+    outs = (attn_out, mlp_out)
+    ins = (attn_ref, mlp_ref)
+
+    def block(group, dev):
+        kind, first, count = GATHER_GROUPS[group]
+        return outs[kind].at[pl.ds(first, count), pl.ds(pl.multiple_of(dev * rows, rows), rows), :]
+
+    def own(group):
+        kind, first, count = GATHER_GROUPS[group]
+        return ins[kind].at[pl.ds(first, count)]
+
+    def ring_copy(group, way, hop):
+        origin = ring_device((place + chips - (hop - 1)) % chips if way == 0 else (place + hop - 1) % chips, core, chips)
+        src = own(group) if hop == 1 else block(group, origin)
+        return remote(
+            src, block(group, origin), ring_send.at[group, way, hop - 1], ring_recv.at[group, way, hop - 1],
+            right if way == 0 else left,
+        )
+
+    def arrived(group, way, hop):
+        origin = (place + 2 * chips - hop) % chips if way == 0 else (place + hop) % chips
+        return ring_device(origin, core, chips)
+
+    def pair_copy(group, slot, dev, first):
+        src = own(group) if first else block(group, dev)
+        return remote(src, block(group, dev), pair_send.at[group, slot], pair_recv.at[group, slot], pair)
+
+    def await_ring(group, way, hop):
+        here = block(group, arrived(group, way, hop))
+        remote(here, here, ring_send.at[group, way, hop - 1], ring_recv.at[group, way, hop - 1], right).wait_recv()
+
+    def await_pair(group):
+        counts = hops(group, chips)
+        pair_copy(group, 0, pair_index, False).wait_recv()
+        for way in (0, 1):
+            for hop in range(1, counts[way] + 1):
+                dev = arrived(group, way, hop) + 1 - 2 * core
+                pair_copy(group, hop if way == 0 else counts[0] + hop, dev, False).wait_recv()
+
+    pair_index = index + 1 - 2 * core
+    sent = []
+    groups = range(len(GATHER_GROUPS))
+    for group in groups:
+        for way in (0, 1):
+            copy = ring_copy(group, way, 1)
+            copy.start()
+            sent.append(copy)
+    for group in groups:
+        copy = pltpu.make_async_copy(own(group), block(group, index), own_sem.at[group])
+        copy.start()
+        sent.append(("own", copy))
+        copy = pair_copy(group, 0, index, True)
+        copy.start()
+        sent.append(copy)
+    longest = chips // 2
+    for hop in range(1, longest + 1):
+        for group in groups:
+            counts = hops(group, chips)
+            for way in (0, 1):
+                if hop > counts[way]:
+                    continue
+                await_ring(group, way, hop)
+                dev = arrived(group, way, hop)
+                if hop < counts[way]:
+                    copy = ring_copy(group, way, hop + 1)
+                    copy.start()
+                    sent.append(copy)
+                slot = hop if way == 0 else counts[0] + hop
+                copy = pair_copy(group, slot, dev, False)
+                copy.start()
+                sent.append(copy)
+            if group == 1 and hop == longest:
+                await_pair(group)
+                own_wait = [c for c in sent if isinstance(c, tuple)][1]
+                own_wait[1].wait()
+                sent = [c for c in sent if c is not own_wait]
+                wo_copy = remote(attn_out.at[3], wo_out, wo_send, wo_recv, across)
+                wo_copy.start()
+    for group in groups:
+        if group == 1:
+            continue
+        await_pair(group)
+    for copy in sent:
+        if isinstance(copy, tuple):
+            copy[1].wait()
+        else:
+            copy.wait_send()
+    wo_copy.wait()
+
+
+def gather_weights(attn_low, mlp_low, fsdp):
+    chips = fsdp // 2
+    rows, cols = attn_low.shape[1:]
+    units = mlp_low.shape[2]
+    number = len(GATHER_GROUPS)
+    anyspec = pl.BlockSpec(memory_space=pl.ANY)
+    return pl.pallas_call(
+        functools.partial(gather_kernel, chips),
+        out_shape=(
+            jax.ShapeDtypeStruct((4, rows * fsdp, cols), BF),
+            jax.ShapeDtypeStruct((3, rows * fsdp, units), BF),
+            jax.ShapeDtypeStruct((rows * fsdp, cols), BF),
+        ),
+        in_specs=[anyspec] * 2,
+        out_specs=(anyspec,) * 3,
+        scratch_shapes=[
+            pltpu.SemaphoreType.DMA((number, 2, chips // 2)),
+            pltpu.SemaphoreType.DMA((number, 2, chips // 2)),
+            pltpu.SemaphoreType.DMA((number, chips)),
+            pltpu.SemaphoreType.DMA((number, chips)),
+            pltpu.SemaphoreType.DMA((number,)),
+            pltpu.SemaphoreType.DMA,
+            pltpu.SemaphoreType.DMA,
+        ],
+        compiler_params=pltpu.CompilerParams(collective_id=1, has_side_effects=True),
+        name="gather_weights",
+    )(attn_low, mlp_low)
+
+
+def scatter_kernel(chips, attn_ref, wu_ref, wg_ref, wd_ref, attn_out, mlp_out, near_attn, near_mlp, first_attn, first_mlp, ring_attn, ring_mlp,
+                   pair_send, pair_recv, ring_send, ring_recv):
+    index, x = lax.axis_index("fsdp"), lax.axis_index("mp")
+    place, core = ring_place(index, chips)
+    right = (ring_device((place + 1) % chips, core, chips), x)
+    left = (ring_device((place + chips - 1) % chips, core, chips), x)
+    pair = (index + 1 - 2 * core, x)
+    greet((right, left, pair))
+    owns = (wu_ref, wg_ref, wd_ref, attn_ref)
+
+    def mine(group, dev):
+        if group == 3:
+            return attn_ref.at[:, dev]
+        return owns[group].at[dev]
+
+    def near(group, chip):
+        if group == 3:
+            return near_attn.at[:, chip]
+        return near_mlp.at[group, chip]
+
+    def first(group, way):
+        return first_attn.at[way] if group == 3 else first_mlp.at[group, way]
+
+    def slot(group, way, hop):
+        if group == 3:
+            return ring_attn.at[way, hop - 1]
+        return ring_mlp.at[group, way, hop - 1]
+
+    order = (2, 0, 1, 3)
+    pairs = {}
+    for group in order:
+        for chip in range(chips):
+            dev = chip * 2 + 1 - core
+            copy = remote(mine(group, dev), near(group, chip), pair_send.at[group, chip], pair_recv.at[group, chip], pair)
+            copy.start()
+            pairs[group, chip] = copy
+
+    def add_into(group, dst, dev, extra):
+        src_a, src_b = mine(group, dev), near(group, dev // 2)
+        rows = src_a.shape[-2]
+        if group == 3:
+            for j in range(src_a.shape[0]):
+                total = src_a[j].astype(F32) + src_b[j].astype(F32)
+                for other in extra:
+                    total = total + other[j].astype(F32)
+                dst[j] = total.astype(dst.dtype)
+        else:
+            step = 16
+            def body(i, _):
+                r = pl.ds(pl.multiple_of(i * step, step), step)
+                total = src_a[r].astype(F32) + src_b[r].astype(F32)
+                for other in extra:
+                    total = total + other[r].astype(F32)
+                dst[r] = total.astype(dst.dtype)
+                return 0
+            lax.fori_loop(0, rows // step, body, 0)
+
+    def target(way, count):
+        return ring_device((place + count) % chips if way == 0 else (place + 2 * chips - count) % chips, core, chips)
+
+    sends = []
+    for group in order:
+        counts = hops(group, chips)
+        for chip in range(chips):
+            pairs[group, chip].wait()
+        for way in (0, 1):
+            dev = target(way, counts[way])
+            add_into(group, first(group, way), dev, ())
+            copy = remote(first(group, way), slot(group, way, 1), ring_send.at[group, way, 0], ring_recv.at[group, way, 0], right if way == 0 else left)
+            copy.start()
+            sends.append(copy)
+    for hop in range(1, chips // 2 + 1):
+        for group in order:
+            counts = hops(group, chips)
+            for way in (0, 1):
+                if hop > counts[way]:
+                    continue
+                here = slot(group, way, hop)
+                remote(here, here, ring_send.at[group, way, hop - 1], ring_recv.at[group, way, hop - 1], right if way == 0 else left).wait_recv()
+                if hop < counts[way]:
+                    dev = target(way, counts[way] - hop)
+                    add_into(group, here, dev, (here,))
+                    copy = remote(here, slot(group, way, hop + 1), ring_send.at[group, way, hop], ring_recv.at[group, way, hop], right if way == 0 else left)
+                    copy.start()
+                    sends.append(copy)
+            if hop == chips // 2:
+                extra = (slot(group, 0, counts[0]), slot(group, 1, counts[1]))
+                dst = attn_out if group == 3 else mlp_out.at[group]
+                add_into(group, dst, index, extra)
+    for copy in sends:
+        copy.wait_send()
+
+
+def scatter_grads(attn_grad, wu, wg, wd, fsdp):
+    chips = fsdp // 2
+    number, width, cols = attn_grad.shape
+    rows, units = width // fsdp, wu.shape[1]
+    vspec = pl.BlockSpec(memory_space=VM)
+    return pl.pallas_call(
+        functools.partial(scatter_kernel, chips),
+        out_shape=(
+            jax.ShapeDtypeStruct((number, rows, cols), F32),
+            jax.ShapeDtypeStruct((3, rows, units), F32),
+        ),
+        in_specs=[vspec] * 4,
+        out_specs=(vspec,) * 2,
+        scratch_shapes=[
+            VM((number, chips, rows, cols), BF),
+            VM((3, chips, rows, units), BF),
+            VM((2, number, rows, cols), BF),
+            VM((3, 2, rows, units), BF),
+            VM((2, chips // 2, number, rows, cols), BF),
+            VM((3, 2, chips // 2, rows, units), BF),
+            pltpu.SemaphoreType.DMA((4, chips)),
+            pltpu.SemaphoreType.DMA((4, chips)),
+            pltpu.SemaphoreType.DMA((4, 2, chips // 2)),
+            pltpu.SemaphoreType.DMA((4, 2, chips // 2)),
+        ],
+        compiler_params=pltpu.CompilerParams(collective_id=2, has_side_effects=True, vmem_limit_bytes=60 * MIB),
+        name="scatter_grads",
+    )(
+        attn_grad.reshape(number, fsdp, rows, cols),
+        *(w.reshape(fsdp, rows, units) for w in (wu, wg, wd)),
+    )
+
+
+def update_kernel(stages, rate, width, ga, gm, small, wa, ma, aa, wm, mm, am, ma_o, wa_o, aa_o, mm_o, wm_o, am_o, small_o, mine, got, send, recv):
+    index, x = lax.axis_index("fsdp"), lax.axis_index("mp")
+    peers = [(index + (1 << s) * (1 - 2 * ((index // (1 << s)) % 2)), x) for s in range(stages)]
+    greet(peers)
+    rows = ga.shape[1]
+    cols, units = ga.shape[2], gm.shape[2]
+
+    def step(j, r, g, w, m, m_o, w_o):
+        grad = g[j, r]
+        moment = MOMENTUM * m[j, r] + grad
+        stepped = w[j, r] - rate * (grad + MOMENTUM * moment)
+        m_o[j, r] = moment
+        w_o[j, r] = stepped
+        return stepped * stepped
+
+    lanes = mine.shape[2]
+
+    def spots(base, count):
+        size = min(count, lanes)
+        return [((base + k) // lanes, (base + k) % lanes, k, size) for k in range(0, count, size)]
+
+    def pack(refs, j, count, base):
+        def body(i, total):
+            r = pl.ds(pl.multiple_of(i * 8, 8), 8)
+            return total + step(j, r, *refs)
+
+        total = jnp.sum(lax.fori_loop(0, rows // 8, body, jnp.zeros((8, count), F32)), axis=0, keepdims=True)
+        for row, lane, k, size in spots(base, count):
+            mine[0, row : row + 1, lane : lane + size] = total[:, k : k + size]
+
+    for j in range(4):
+        pack((ga, wa, ma, ma_o, wa_o), j, cols, j * cols)
+    for j in range(3):
+        pack((gm, wm, mm, mm_o, wm_o), j, units, 4 * cols + j * units)
+    squares = (4 * cols + 3 * units) // lanes
+    mine[0, squares:] = small[...]
+    for s in range(stages):
+        copy = remote(mine.at[s], got.at[s], send.at[s], recv.at[s], peers[s])
+        copy.start()
+        copy.wait()
+        mine[s + 1] = mine[s] + got[s]
+    small_o[...] = mine[stages, squares:]
+
+    def finish(j, count, base, a, a_o, w_o):
+        for row, lane, k, size in spots(base, count):
+            c = slice(k, k + size)
+            scale = lax.rsqrt(mine[stages, row : row + 1, lane : lane + size] / width + EPS)
+
+            def body(i, _):
+                r = pl.ds(pl.multiple_of(i * 8, 8), 8)
+                new = w_o[j, r, c] * scale
+                w_o[j, r, c] = new
+                a_o[j, r, c] = AVERAGE * a[j, r, c] + (1.0 - AVERAGE) * new
+                return 0
+
+            lax.fori_loop(0, rows // 8, body, 0)
+
+    for j in range(4):
+        finish(j, cols, j * cols, aa, aa_o, wa_o)
+    for j in range(3):
+        finish(j, units, 4 * cols + j * units, am, am_o, wm_o)
+
+
+def update(ga, gm, small, wa, ma, aa, wm, mm, am, rate, width, fsdp):
+    stages = fsdp.bit_length() - 1
+    lanes = small.shape[1]
+    squares = (4 * wa.shape[2] + 3 * wm.shape[2]) // lanes
+    total = squares + small.shape[0]
+    vspec = pl.BlockSpec(memory_space=VM)
+    a_shape, m_shape = jax.ShapeDtypeStruct(wa.shape, F32), jax.ShapeDtypeStruct(wm.shape, F32)
+    return pl.pallas_call(
+        functools.partial(update_kernel, stages, rate, width),
+        out_shape=(a_shape, a_shape, a_shape, m_shape, m_shape, m_shape, jax.ShapeDtypeStruct(small.shape, F32)),
+        in_specs=[vspec] * 9,
+        out_specs=(vspec,) * 7,
+        scratch_shapes=[
+            VM((stages + 1, total, lanes), F32),
+            VM((stages, total, lanes), F32),
+            pltpu.SemaphoreType.DMA((stages,)),
+            pltpu.SemaphoreType.DMA((stages,)),
+        ],
+        compiler_params=pltpu.CompilerParams(collective_id=3, has_side_effects=True, vmem_limit_bytes=60 * MIB),
+        name="update_weights",
+    )(ga, gm, small, wa, ma, aa, wm, mm, am)
 
 
 def local(
@@ -301,7 +702,199 @@
     )
 
 
+def local_fast(
+    inputs,
+    doc_ids,
+    out_grad,
+    attn_w,
+    attn_mom,
+    attn_avg,
+    mlp_w,
+    mlp_mom,
+    mlp_avg,
+    head_scale,
+    head_mom,
+    mix_rates,
+    mix_mom,
+    unit_scales,
+    unit_mom,
+):
+    length = inputs.shape[1]
+    model_width = inputs.shape[2]
+    head_count = head_scale.shape[0] // HD
+    block_rows = min(512, length)
+    block_count = length // block_rows
+    tokens = inputs.shape[0] * lax.axis_size("fsdp") * length
+    doc_row = doc_ids[0]
+    input_low = inputs[0]
+    resid_in = input_low.astype(jnp.float32)
+    cos_table, sin_table = rotary_tables(doc_row)
+    position = jnp.arange(length, dtype=jnp.int32)
+    fsdp = lax.axis_size("fsdp")
+    attn_full, mlp_full, _ = gather_weights(attn_w.astype(BF), mlp_w.astype(BF), fsdp)
+    attn_back, mlp_back = attn_full, mlp_full
+    projected = jnp.einsum(
+        "sd,jdc->jsc", input_low, attn_full[:3], preferred_element_type=jnp.float32
+    )
+    head_gain = head_scale.reshape(head_count, HD)
+    q_rot = rotate(projected[0].reshape(length, head_count, HD), cos_table, sin_table)
+    k_rot = rotate(projected[1].reshape(length, head_count, HD), cos_table, sin_table)
+    q_unit = rms_unit(q_rot)
+    k_unit = rms_unit(k_rot)
+    query_low = (head_gain * q_unit).astype(jnp.bfloat16)
+    key_low = (head_gain * k_unit).astype(jnp.bfloat16)
+    value_low = projected[2].reshape(length, head_count, HD).astype(jnp.bfloat16)
+
+    def scores_of(row_first):
+        query_blk = lax.dynamic_slice_in_dim(query_low, row_first, block_rows, 0)
+        raw_scores = jnp.einsum(
+            "qhe,khe->hqk", query_blk, key_low, preferred_element_type=jnp.float32
+        )
+        row_pos = lax.dynamic_slice_in_dim(position, row_first, block_rows, 0)
+        row_docs = lax.dynamic_slice_in_dim(doc_row, row_first, block_rows, 0)
+        allowed = (row_docs[:, None] == doc_row[None, :]) & (position[None, :] <= row_pos[:, None])
+        return (jnp.where(allowed[None], raw_scores * HD ** (-0.5), NEG_FILL), query_blk)
+
+    def attend(accums, blk_index):
+        scores, query_blk = scores_of(blk_index * block_rows)
+        peak_val = jnp.max(scores, axis=-1, keepdims=True)
+        expo_vals = jnp.exp(scores - peak_val)
+        row_total = jnp.sum(expo_vals, axis=-1, keepdims=True)
+        probs_low = (expo_vals / row_total).astype(jnp.bfloat16)
+        blk_out = jnp.einsum(
+            "hqk,khe->qhe", probs_low, value_low, preferred_element_type=jnp.float32
+        )
+        return (accums, (blk_out, (peak_val + jnp.log(row_total))[..., 0]))
+
+    _, (mixed_blocks, log_totals) = lax.scan(attend, None, jnp.arange(block_count))
+    mixed_low = mixed_blocks.reshape(length, head_count * HD).astype(jnp.bfloat16)
+    attn_part = jnp.einsum("sc,dc->sd", mixed_low, attn_full[3], preferred_element_type=jnp.float32)
+    attn_out = lax.psum(attn_part, "mp")
+    attn_unit = rms_unit(attn_out)
+    resid_one = resid_in + mix_rates[0] * (attn_unit - resid_in)
+    hidden_one = rms_unit(resid_one)
+    hidden_low = hidden_one.astype(jnp.bfloat16)
+    gates = jnp.einsum("sd,jdf->jsf", hidden_low, mlp_full[:2], preferred_element_type=jnp.float32)
+    up_proj = gates[0]
+    gate_proj = gates[1]
+    gate_arg = unit_scales[1] * gate_proj * D ** (-0.5)
+    gate_sig = jax.nn.sigmoid(gate_arg)
+    gate_act = gate_arg * gate_sig
+    units_low = (unit_scales[0] * up_proj * gate_act).astype(jnp.bfloat16)
+    mlp_part = jnp.einsum("sf,df->sd", units_low, mlp_full[2], preferred_element_type=jnp.float32)
+    mlp_out = lax.psum(mlp_part, "mp")
+    mlp_unit = rms_unit(mlp_out)
+    resid_two = hidden_one + mix_rates[1] * (mlp_unit - hidden_one)
+    result = rms_unit(resid_two)
+    cotangent = out_grad[0].astype(jnp.float32)
+    d_resid_two = rms_back(resid_two, cotangent)
+    grad_mix_mlp = jnp.sum(d_resid_two * (mlp_unit - hidden_one), axis=0)
+    d_hidden_one = d_resid_two * (1.0 - mix_rates[1])
+    d_mlp_low = rms_back(mlp_out, mix_rates[1] * d_resid_two).astype(jnp.bfloat16)
+    d_units = jnp.einsum("sd,df->sf", d_mlp_low, mlp_back[2], preferred_element_type=jnp.float32)
+    d_up = d_units * unit_scales[0] * gate_act
+    d_arg = d_units * unit_scales[0] * up_proj * gate_sig * (1.0 + gate_arg * (1.0 - gate_sig))
+    d_gate = d_arg * unit_scales[1] * D ** (-0.5)
+    grad_units = jnp.stack(
+        [
+            jnp.sum(d_units * up_proj * gate_act, axis=0),
+            jnp.sum(d_arg * gate_proj * D ** (-0.5), axis=0),
+        ]
+    )
+    d_gates_low = jnp.stack([d_up, d_gate]).astype(jnp.bfloat16)
+    mlp_back_part = jnp.einsum(
+        "jsf,jdf->sd", d_gates_low, mlp_back[:2], preferred_element_type=jnp.float32
+    )
+    d_hidden_one = d_hidden_one + lax.psum(mlp_back_part, "mp")
+    w_u = jnp.einsum("sd,sf->df", hidden_low, d_gates_low[0], preferred_element_type=jnp.float32).astype(BF)
+    w_g = jnp.einsum("sd,sf->df", hidden_low, d_gates_low[1], preferred_element_type=jnp.float32).astype(BF)
+    w_d = jnp.einsum("sd,sf->df", d_mlp_low, units_low, preferred_element_type=jnp.float32).astype(BF)
+    d_resid_one = rms_back(resid_one, d_hidden_one)
+    grad_mix_attn = jnp.sum(d_resid_one * (attn_unit - resid_in), axis=0)
+    d_resid_in = d_resid_one * (1.0 - mix_rates[0])
+    d_attn_low = rms_back(attn_out, mix_rates[0] * d_resid_one).astype(jnp.bfloat16)
+    d_mixed = jnp.einsum("sd,dc->sc", d_attn_low, attn_back[3], preferred_element_type=jnp.float32)
+    d_mixed = d_mixed.astype(jnp.bfloat16).reshape(length, head_count, HD)
+
+    def attend_back(accums, blk_index):
+        d_key, d_value = accums
+        row_first = blk_index * block_rows
+        scores, query_blk = scores_of(row_first)
+        blk_total = lax.dynamic_index_in_dim(log_totals, blk_index, 0, keepdims=False)
+        attn_probs = jnp.exp(scores - blk_total[..., None])
+        d_out_blk = lax.dynamic_slice_in_dim(d_mixed, row_first, block_rows, 0)
+        d_probs = jnp.einsum(
+            "qhe,khe->hqk", d_out_blk, value_low, preferred_element_type=jnp.float32
+        )
+        d_scores = attn_probs * (d_probs - jnp.sum(attn_probs * d_probs, axis=-1, keepdims=True))
+        d_raw_low = (d_scores * HD ** (-0.5)).astype(jnp.bfloat16)
+        d_query = jnp.einsum("hqk,khe->qhe", d_raw_low, key_low, preferred_element_type=jnp.float32)
+        d_key = d_key + jnp.einsum(
+            "hqk,qhe->khe", d_raw_low, query_blk, preferred_element_type=jnp.float32
+        )
+        d_value = d_value + jnp.einsum(
+            "hqk,qhe->khe",
+            attn_probs.astype(jnp.bfloat16),
+            d_out_blk,
+            preferred_element_type=jnp.float32,
+        )
+        return ((d_key, d_value), d_query)
+
+    zero_heads = jnp.zeros((length, head_count, HD), jnp.float32)
+    (d_key_all, d_value_all), d_query_blocks = lax.scan(
+        attend_back, (zero_heads, zero_heads), jnp.arange(block_count)
+    )
+    d_query_all = d_query_blocks.reshape(length, head_count, HD)
+    grad_head = jnp.sum(d_query_all * q_unit + d_key_all * k_unit, axis=0).reshape(-1)
+    d_query_raw = rotate_back(rms_back(q_rot, head_gain * d_query_all), cos_table, sin_table)
+    d_key_raw = rotate_back(rms_back(k_rot, head_gain * d_key_all), cos_table, sin_table)
+    d_proj_low = jnp.stack(
+        [
+            d_query_raw.reshape(length, -1),
+            d_key_raw.reshape(length, -1),
+            d_value_all.reshape(length, -1),
+        ]
+    ).astype(jnp.bfloat16)
+    grad_mix = jnp.stack([grad_mix_attn, grad_mix_mlp])
+    attn_back_part = jnp.einsum(
+        "jsc,jdc->sd", d_proj_low, attn_back[:3], preferred_element_type=jnp.float32
+    )
+    input_grad = d_resid_in + lax.psum(attn_back_part.astype(jnp.bfloat16), "mp").astype(
+        jnp.float32
+    )
+    in_terms = jnp.einsum("sd,jsc->jdc", input_low, d_proj_low, preferred_element_type=jnp.float32)
+    out_terms = jnp.einsum("sd,sc->dc", d_attn_low, mixed_low, preferred_element_type=jnp.float32)
+    w_a = jnp.concatenate([in_terms, out_terms[None]], 0).astype(BF)
+    grad_attn, grad_mlp = scatter_grads(w_a, w_u, w_g, w_d, fsdp)
+    root_tokens = math.sqrt(tokens)
+    weight_rate = RATE_WEIGHT / root_tokens
+    small = jnp.concatenate([jnp.pad(grad_head, (0, D - grad_head.shape[0])), grad_mix.reshape(-1), grad_units.reshape(-1), jnp.zeros((D,), F32)]).reshape(8, D)
+    attn_mom_new, attn_new, attn_avg_new, mlp_mom_new, mlp_new, mlp_avg_new, small = update(
+        grad_attn, grad_mlp, small, attn_w, attn_mom, attn_avg, mlp_w, mlp_mom, mlp_avg, weight_rate, model_width, fsdp)
+    grad_head, grad_mix, grad_units = small[0, : grad_head.shape[0]], small[1:3], small[3:7].reshape(2, -1)
+    head_mom_new, head_new = nesterov(head_scale, head_mom, grad_head, RATE_HEAD / root_tokens)
+    mix_mom_new, mix_new = nesterov(mix_rates, mix_mom, grad_mix, RATE_MIX / root_tokens)
+    units_mom_new, units_new = nesterov(unit_scales, unit_mom, grad_units, RATE_UNITS / root_tokens)
+    return (
+        result[None],
+        input_grad[None],
+        attn_mom_new,
+        attn_new,
+        attn_avg_new,
+        mlp_mom_new,
+        mlp_new,
+        mlp_avg_new,
+        head_mom_new,
+        head_new,
+        mix_mom_new,
+        mix_new,
+        units_mom_new,
+        units_new,
+    )
+
+
 def solution(mesh):
+    fast = D // mesh.shape["fsdp"] % 16 == 0 and mesh.shape["fsdp"] % 8 == 0
     placed = (
         P("fsdp", None, None),
         P("fsdp", None),
@@ -320,7 +913,7 @@
         P(None, "mp"),
     )
     return jax.shard_map(
-        local,
+        local_fast if fast else local,
         mesh=mesh,
         in_specs=placed,
         out_specs=(

time: 1450 us -> 989 us (0.68)
  waiting for transfers between devices: 857 us -> 280 us
  Pallas kernels: 0 us -> 223 us
  blocking collectives: 60.4 us -> 0 us
  other arithmetic: 109 us -> 80.4 us
  local copies, waits for them, and re-layouts: 111 us -> 94.4 us
    reduce_scatter x1 -> x0, waiting for transfers between devices: 245 us -> none  [local(): lax.psum_scatter(jnp.concatenate([jnp.einsum('sd,jsf->djf', left_cols, d_...]
    pallas_call x0 -> x3, Pallas kernels: none -> 223 us  [the longest x1 104 us: gather_weights(): pl.pallas_call(functools.partial(gather_kernel, chips), out_shape=(jax.Sh...]
    unnamed x9 -> x4, waiting for transfers between devices: 154 us -> 0.07 us
    all_gather x2 -> x0, waiting for transfers between devices: 147 us -> none  [the longest x1 95.4 us: local(): lax.all_gather(mlp_w.astype(jnp.bfloat16), 'fsdp', axis=1, tiled=True)]
    psum x1 -> x0, blocking collectives: 60.4 us -> none  [local(): attn_squares, mlp_squares = lax.psum((attn_squares, mlp_squares), 'fsdp')]
    psum x4, waiting for transfers between devices: 311 us -> 280 us  [the longest x1 107 us: local_fast(): attn_out = lax.psum(attn_part, 'mp')]
    concatenate x2, other arithmetic: 22.8 us -> 2.35 us  [the longest x1 2.35 us: local_fast(): w_a = jnp.concatenate([in_terms, out_terms[None]], 0).astype(BF)]
    unnamed x198 -> x164, local copies, waits for them, and re-layouts: 33.8 us -> 20.9 us
  transfers between devices with their start and end apart: 8 -> 4, of which waited for: 7 -> 3; matrix products, arithmetic and copies ran while one was open for 7% -> 7% of each run, Pallas kernels for 0% -> 12%
where the time goes in v1:
time: 989 us; the launch traced here: 979 us
  waiting for transfers between devices  280 us (28%)
  matrix products  279 us (28%)
  Pallas kernels  223 us (23%)
  local copies, waits for them, and re-layouts  94.4 us (10%)
  other arithmetic  80.4 us (8%)
  between operations  15.1 us (2%)
    psum x1, waiting for transfers between devices, local_fast(): attn_out = lax.psum(attn_part, 'mp')  107 us
    pallas_call x1, Pallas kernels, gather_weights(): pl.pallas_call(functools.partial(gather_kernel, chips), out_shape=(jax.Sh...  104 us
    psum x1, waiting for transfers between devices, local_fast(): mlp_out = lax.psum(mlp_part, 'mp')  102 us
    pallas_call x1, Pallas kernels, scatter_grads(): pl.pallas_call(functools.partial(scatter_kernel, chips), out_shape=(jax.S...  95.6 us
    psum x1, waiting for transfers between devices, local_fast(): d_hidden_one = d_hidden_one + lax.psum(mlp_back_part, 'mp')  71.3 us
    dot_general x2, matrix products, attend_back(): jnp.einsum('hqk,khe->qhe', d_raw_low, key_low, preferred_element_type=jnp...  50.8 us
    dot_general x2, matrix products, attend_back(): jnp.einsum('hqk,qhe->khe', d_raw_low, query_blk, preferred_element_type=j...  47.5 us
    dynamic_update_slice x4, local copies, waits for them, and re-layouts, local_fast(): lax.scan(attend, None, jnp.arange(block_count))  43.6 us
  transfers between devices with their start and end apart: 4, of which 3 were waited for; matrix products, arithmetic and copies ran while one was open for 7% of the time, Pallas kernels for 12%

profile of v1, /device:TPU:0, one launch (start us, length us, event | category | flops | bytes accessed | tf_op | source)
XLA Modules:
  0.0 979.3 jit_solution(11218436808231526384)
XLA Ops:
  11.6 104.2 %gather_weights.1 = (bf16[4,1024,512]{2,1,0:T(8,128)(2,1)}, bf16[3,1024,2048]{2,1,0:T(8,128)(2,1)}, bf16[1024,512]{1,0:T(8,128)(2,1)}) custom-call(bf16[4,64,512]{2,1,0:T(8,128)(2,1)} %convert_element_type.94.attn_ref, bf16[3,64,2048]{2,1,0:T(8,128)(2,1)} %convert_element_type.95.mlp_ref), custom_call_target="tpu_custom_call" | custom-call | tf_op jit(solution)/shard_map/gather_weights/pallas_call | solution.py:247
  129.4 31.5 %while.29 = (s32[]{:T(128)}, bf16[2,512,8,64]{1,3,2,0:T(8,128)(2,1)S(1)}, f32[2,8,512]{2,1,0:T(8,128)S(1)}, s32[2]{0:T(128)S(1)}, s32[1024]{0:T(1024)S(1)}, /*in...) while((s32[]{:T(128)}, ...), condition=%wide.region_7.8_spmd.clone, body=%wide.region_4.7_spmd.clone.sunk | while | flops 1125642240 | bytes 56250584 | solution.py:769
  169.2 106.7 %all-reduce.6.cloned.1.call-done = f32[1024,1024]{1,0:T(8,128)} async-done(((f32[1024,1024]{1,0:T(8,128)}), f32[1024,1024]{1,0:T(8,128)}) %all-reduce.6.cloned.1.call-update) | async-done | bytes 4194320 | tf_op jit(solution)/shard_map/psum | solution.py:772
  286.1 12.3 %fusion.61 = f32[2,1024,2048]{2,1,0:T(8,128)} fusion(bf16[3,1024,2048]{2,1,0:T(8,128)(2,1)S(1)} %copy-done.76, bf16[1024,1024]{1,0:T(8,128)(2,1)S(1)} %multiply_convert_fusion.7), kind=kOutput, calls=%fused_computation.70 | convolution fusion | flops 8589934592 | bytes 27262976 | tf_op jit(solution)/shard_map/sd,jdf->jsf/dot_general | solution.py:777
  298.5 10.5 %fusion.70 = f32[1024,1024]{1,0:T(8,128)} fusion(f32[2,1024,2048]{2,1,0:T(8,128)} %fusion.61, f32[2048]{0:T(1024)S(1)} %bitcast.270, f32[2048]{0:T(1024)S(1)} %bitcast.279, bf16[3,1024,2048]{2,1,0:T(8,128)(2,1)S(1)} %copy-done.76), kind=kOutput, calls=%fused_computation.82 | convolution fusion | flops 4313841664 | bytes 25182208 | tf_op jit(solution)/shard_map/sf,df->sd/dot_general | solution.py:784
  314.6 102.5 %all-reduce.8.cloned.1.call-done = f32[1024,1024]{1,0:T(8,128)} async-done(((f32[1024,1024]{1,0:T(8,128)}), f32[1024,1024]{1,0:T(8,128)}) %all-reduce.8.cloned.1.call-update) | async-done | bytes 4194320 | tf_op jit(solution)/shard_map/psum | solution.py:785
  429.5 17.5 %fusion.53 = (f32[2048]{0:T(1024)S(1)}, f32[2048]{0:T(1024)S(1)}, f32[1024,2048]{1,0:T(8,128)}, bf16[1024,2048]{1,0:T(8,128)(2,1)S(1)}) fusion(f32[2,1024,2048]{2,1,0:T(8,128)} %fusion.61, f32[2048]{0:T(1024)S(1)} %bitcast.271, f32[2048]{0:T(1024)S(1)} %bitcast.280, bf16[3,1024,2048]{2,1,0:T(8,128)(2,1)} %get-tuple-element.155, ...), kind=kOutput, calls=%fused_computation.56 | convolution fusion | flops 4354732032 | bytes 44097536 | tf_op jit(solution)/shard_map/sd,df->sf/dot_general | solution.py:794
  453.0 12.6 %fusion.81 = f32[1024,1024]{1,0:T(8,128)} fusion(bf16[3,1024,2048]{2,1,0:T(8,128)(2,1)} %get-tuple-element.155, bf16[1,1024,2048]{2,1,0:T(8,128)(2,1)S(1)} %fusion.95, bf16[1,1024,2048]{2,1,0:T(8,128)(2,1)S(1)} %bitcast.284), kind=kOutput, calls=%fused_computation.114 | convolution fusion | flops 8594128896 | bytes 20971520 | tf_op jit(solution)/shard_map/jsf,jdf->sd/dot_general | solution.py:805
  465.7 9.5 convolution_convert_fusion.1
  475.8 10.2 %convolution_convert_fusion = bf16[1024,2048]{1,0:T(8,128)(2,1)} fusion(bf16[1024,1024]{1,0:T(8,128)(2,1)S(1)} %copy-done.33, f32[1024,2048]{1,0:T(8,128)} %get-tuple-element.325, f32[2048]{0:T(1024)S(1)} %bitcast.273), kind=kOutput, calls=%fused_computation.102 | convolution fusion | flops 4303355904 | bytes 14688256 | tf_op jit(solution)/shard_map/sd,sf->df/dot_general | solution.py:810
  486.0 16.3 %fusion.74 = bf16[1024,2048]{1,0:T(8,128)(2,1)} fusion(f32[2,1024,2048]{2,1,0:T(8,128)} %fusion.61, f32[2048]{0:T(1024)S(1)} %bitcast.281, f32[2048]{0:T(1024)S(1)} %bitcast.274, f32[1024,1024]{1,0:T(8,128)} %all-reduce.8.cloned.1.call-done, bf16[1,1024,1024]{2,1,0:T(8,128)(2,1)S(1)} %copy-done.14, f32[1024]{0:T(1024)S(1)} %broadcast_multiply_fusion.3, ...), kind=kOutput, calls=%fused_computation.101 | convolution fusion | flops 4331667456 | bytes 31498240 | tf_op jit(solution)/shard_map/sd,sf->df/dot_general | solution.py:811
  502.3 71.3 %all-reduce.10.cloned.1.call-done = f32[1024,1024]{1,0:T(8,128)} async-done(((f32[1024,1024]{1,0:T(8,128)}), f32[1024,1024]{1,0:T(8,128)}) %all-reduce.10.cloned.1.call-update) | async-done | bytes 4194320 | tf_op jit(solution)/shard_map/psum | solution.py:808
  596.2 192.9 %while.30 = (s32[]{:T(128)}, f32[1024,8,64]{0,2,1:T(8,128)}, f32[1024,8,64]{0,2,1:T(8,128)}, f32[2,512,8,64]{1,0,3,2:T(2,128)}, s32[2]{0:T(128)S(1)}, /*index=5*...) while((s32[]{:T(128)}, f32[1024,8,64]{0,2,1:T(8,128)}, ...), condition=%wide.region_21.22_spmd.clone.clone, body=%wide.region_19.21_spmd.clone.clone.sunk | while | flops 2746755072 | bytes 238096720 | solution.py:844
  612.2 9.2 fusion.160
  621.3 25.4 %fusion.161 = f32[1,512,8,64]{1,3,2,0:T(8,128)} fusion(bf16[1024,8,64]{0,2,1:T(8,128)(2,1)S(1)} %get-tuple-element.591, f32[8,512,1024]{2,1,0:T(8,128)} %copy-done, f32[8,512,1024]{2,1,0:T(8,128)} %fusion.160), kind=kOutput, calls=%fused_computation.29.clone.1 | convolution fusion | flops 557847552 | bytes 35651584 | tf_op jit(solution)/shard_map/while/body/eval_jaxpr/hqk,khe->qhe/dot_general | solution.py:831
  646.7 23.5 %bitcast_add_fusion.4 = f32[1024,8,64]{0,2,1:T(8,128)} fusion(f32[1024,8,64]{0,2,1:T(8,128)} %get-tuple-element.565, f32[8,512,1024]{2,1,0:T(8,128)} %copy-done, f32[8,512,1024]{2,1,0:T(8,128)} %fusion.160, pred[]{:T(512)S(6)} %compare.8, bf16[1024,8,64]{0,2,1:T(8,128)(2,1)} %get-tuple-element.587, s32[]{:T(128)S(6)} %select_n.65), kind=kOutput, calls=%fused_computation.27.clone.1 | convolution fusion | flops 558896128 | bytes 71827464 | tf_op jit(solution)/shard_map/while/body/eval_jaxpr/hqk,qhe->khe/dot_general | solution.py:832
  672.6 19.5 %dynamic_update_slice.22 = f32[2,512,8,64]{1,0,3,2:T(2,128)} dynamic-update-slice(f32[2,512,8,64]{1,0,3,2:T(2,128)} %get-tuple-element.567, f32[1,512,8,64]{1,0,3,2:T(1,128)S(1)} %copy.91, s32[]{:T(128)S(6)} %copy.111, s32[]{:T(128)} %constant.54.clone.1..sunk.1, s32[]{:T(128)} %constant.54.clone.1..sunk.1, s32[]{:T(128)} %constant.54.clone.1..sunk.1) | dynamic-update-slice | bytes 2097156 | tf_op jit(solution)/shard_map/while/body/jit(dynamic_update_index_in_dim)/dynamic_update_slice | solution.py:769
  708.8 9.2 fusion.160
  717.9 25.4 %fusion.161 = f32[1,512,8,64]{1,3,2,0:T(8,128)} fusion(bf16[1024,8,64]{0,2,1:T(8,128)(2,1)S(1)} %get-tuple-element.591, f32[8,512,1024]{2,1,0:T(8,128)} %copy-done, f32[8,512,1024]{2,1,0:T(8,128)} %fusion.160), kind=kOutput, calls=%fused_computation.29.clone.1 | convolution fusion | flops 557847552 | bytes 35651584 | tf_op jit(solution)/shard_map/while/body/eval_jaxpr/hqk,khe->qhe/dot_general | solution.py:831
  743.3 24.0 %bitcast_add_fusion.4 = f32[1024,8,64]{0,2,1:T(8,128)} fusion(f32[1024,8,64]{0,2,1:T(8,128)} %get-tuple-element.565, f32[8,512,1024]{2,1,0:T(8,128)} %copy-done, f32[8,512,1024]{2,1,0:T(8,128)} %fusion.160, pred[]{:T(512)S(6)} %compare.8, bf16[1024,8,64]{0,2,1:T(8,128)(2,1)} %get-tuple-element.587, s32[]{:T(128)S(6)} %select_n.65), kind=kOutput, calls=%fused_computation.27.clone.1 | convolution fusion | flops 558896128 | bytes 71827464 | tf_op jit(solution)/shard_map/while/body/eval_jaxpr/hqk,qhe->khe/dot_general | solution.py:832
  769.6 19.5 %dynamic_update_slice.22 = f32[2,512,8,64]{1,0,3,2:T(2,128)} dynamic-update-slice(f32[2,512,8,64]{1,0,3,2:T(2,128)} %get-tuple-element.567, f32[1,512,8,64]{1,0,3,2:T(1,128)S(1)} %copy.91, s32[]{:T(128)S(6)} %copy.111, s32[]{:T(128)} %constant.54.clone.1..sunk.1, s32[]{:T(128)} %constant.54.clone.1..sunk.1, s32[]{:T(128)} %constant.54.clone.1..sunk.1) | dynamic-update-slice | bytes 2097156 | tf_op jit(solution)/shard_map/while/body/jit(dynamic_update_index_in_dim)/dynamic_update_slice | solution.py:769
  810.8 7.7 bitcast_convert_fusion
  837.9 95.6 %scatter_grads.1 = (f32[4,64,512]{2,1,0:T(8,128)}, f32[3,64,2048]{2,1,0:T(8,128)}) custom-call(bf16[4,16,64,512]{3,2,1,0:T(8,128)(2,1)} %pad_maximum_fusion.attn_ref, bf16[16,64,2048]{2,1,0:T(8,128)(2,1)} %bitcast.240, bf16[16,64,2048]{2,1,0:T(8,128)(2,1)} %bitcast.241, bf16[16,64,2048]{2,1,0:T(8,128)(2,1)} %bitcast.242), custom_call_target="tpu_custom_call" | custom-call | tf_op jit(solution)/shard_map/scatter_grads/pallas_call | solution.py:368
  933.5 22.9 %update_weights.1 = (f32[4,64,512]{2,1,0:T(8,128)}, f32[4,64,512]{2,1,0:T(8,128)}, f32[4,64,512]{2,1,0:T(8,128)}, f32[3,64,2048]{2,1,0:T(8,128)}, f32[3,64,2048]...) custom-call(f32[4,64,512]{2,1,0:T(8,128)} %get-tuple-element.160.ga, f32[3,64,2048]{2,1,0:T(8,128)} %get-tuple-element.161.gm, ...), custom_call_target="tpu_custom_call" | custom-call | tf_op jit(solution)/shard_map/update_weights/pallas_call | solution.py:466
  (296 shorter events, 202.0 us)
Async XLA Ops:
  7.2 108.6 %copy-start.25 = (bf16[1,1024,1024]{2,1,0:T(8,128)(2,1)S(1)}, bf16[1,1024,1024]{2,1,0:T(8,128)(2,1)}, u32[]{:S(2)}) copy-start(bf16[1,1024,1024]{2,1,0:T(8,128)(2,1)} %param.19) | copy-start | bytes 6291460
  7.2 268.7 %all-reduce.6.cloned.1.call-start = ((), (), s32[]{:S(2)}) async-start(), calls=%async_computation | async-start | bytes 8388608 | tf_op jit(solution)/shard_map/psum | solution.py:772
  167.9 110.7 %copy-start.26 = (bf16[1,1024,1024]{2,1,0:T(8,128)(2,1)S(1)}, bf16[1,1024,1024]{2,1,0:T(8,128)(2,1)}, u32[]{:S(2)}) copy-start(bf16[1,1024,1024]{2,1,0:T(8,128)(2,1)} %param.19) | copy-start | bytes 6291460
  167.9 249.2 %all-reduce.8.cloned.1.call-start = ((), (), s32[]{:S(2)}) async-start(), calls=%async_computation.1 | async-start | bytes 8388608 | tf_op jit(solution)/shard_map/psum | solution.py:785
  169.2 111.6 %copy-start.61 = (f32[1,1024]{1,0:T(1,128)}, f32[1,1024]{1,0:T(1,128)S(1)}, u32[]{:S(2)}) copy-start(f32[1,1024]{1,0:T(1,128)S(1)} %get-tuple-element.352) | copy-start | bytes 12292
  283.2 15.3 %copy-start.32 = (bf16[1024,1024]{1,0:T(8,128)(2,1)}, bf16[1024,1024]{1,0:T(8,128)(2,1)S(1)}, u32[]{:S(2)}) copy-start(bf16[1024,1024]{1,0:T(8,128)(2,1)S(1)} %multiply_convert_fusion.7) | copy-start | bytes 6291460
  309.0 264.6 %all-reduce.10.cloned.1.call-start = ((), (), s32[]{:S(2)}) async-start(), calls=%async_computation.2 | async-start | bytes 8388608 | tf_op jit(solution)/shard_map/psum | solution.py:808
  465.6 494.9 %all-reduce.12.cloned.1.call-start = ((), (), s32[]{:S(2)}) async-start(), calls=%async_computation.3 | async-start | bytes 4194304 | tf_op jit(solution)/shard_map/psum | solution.py:862
  465.7 10.1 %copy-start.33 = (bf16[1024,1024]{1,0:T(8,128)(2,1)S(1)}, bf16[1024,1024]{1,0:T(8,128)(2,1)}, u32[]{:S(2)}) copy-start(bf16[1024,1024]{1,0:T(8,128)(2,1)} %copy-done.32) | copy-start | bytes 6291460
  475.8 10.2 %copy-start.3 = (f32[1024,1024]{1,0:T(8,128)S(1)}, f32[1024,1024]{1,0:T(8,128)}, u32[]{:S(2)}) copy-start(f32[1024,1024]{1,0:T(8,128)} %copy-done.1) | copy-start | bytes 12582916
  486.0 87.6 %copy-start.66 = (f32[1,1024]{1,0:T(1,128)S(1)}, f32[1,1024]{1,0:T(1,128)}, u32[]{:S(2)}) copy-start(f32[1,1024]{1,0:T(1,128)} %get-tuple-element.351) | copy-start | bytes 12292
  573.6 8.3 copy-start.10
  573.6 8.9 copy-start.27
  573.6 8.9 copy-start.60
  573.7 8.9 copy-start.62
  792.2 7.9 copy-start.47
  792.2 7.9 copy-start.50
  933.4 24.5 %copy-start.74 = (f32[512]{0:T(512)S(1)}, f32[512]{0:T(512)}, u32[]{:S(2)}) copy-start(f32[512]{0:T(512)} %param.28) | copy-start | bytes 6148
  933.4 24.5 %copy-start.75 = (f32[512]{0:T(512)S(1)}, f32[512]{0:T(512)}, u32[]{:S(2)}) copy-start(f32[512]{0:T(512)} %param.29) | copy-start | bytes 6148
  933.5 25.0 %copy-start.68 = (f32[2,1024]{1,0:T(2,128)S(1)}, f32[2,1024]{1,0:T(2,128)}, u32[]{:S(2)}) copy-start(f32[2,1024]{1,0:T(2,128)} %param.30) | copy-start | bytes 24580
  933.5 25.0 %copy-start.72 = (f32[2,1024]{1,0:T(2,128)S(1)}, f32[2,1024]{1,0:T(2,128)}, u32[]{:S(2)}) copy-start(f32[2,1024]{1,0:T(2,128)} %param.31) | copy-start | bytes 24580
  933.5 26.4 %copy-start.64 = (f32[2,2048]{1,0:T(2,128)S(1)}, f32[2,2048]{1,0:T(2,128)}, u32[]{:S(2)}) copy-start(f32[2,2048]{1,0:T(2,128)} %param.32) | copy-start | bytes 49156
  933.5 26.4 %copy-start.71 = (f32[2,2048]{1,0:T(2,128)S(1)}, f32[2,2048]{1,0:T(2,128)}, u32[]{:S(2)}) copy-start(f32[2,2048]{1,0:T(2,128)} %param.33) | copy-start | bytes 49156
  933.5 27.0 %copy-start.70 = (f32[1,1024]{1,0:T(1,128)S(1)}, f32[1,1024]{1,0:T(1,128)}, u32[]{:S(2)}) copy-start(f32[1,1024]{1,0:T(1,128)} %get-tuple-element.350) | copy-start | bytes 12292
  (59 other events, 251.6 us)
Sparse Core Ops, SparseCore 0:
  168.0 107.7 all-reduce.5
  309.2 107.8 all-reduce.7
  465.7 107.8 all-reduce.9
  818.7 62.9 all-reduce.11

commit v2 on v1

--- a/solution.py
+++ b/solution.py
@@ -479,6 +479,517 @@
     )(ga, gm, small, wa, ma, aa, wm, mm, am)
 
 
+BLOCK = 256
+SPAN = 512
+
+
+def head_ones():
+    row = lax.broadcasted_iota(jnp.int32, (128, 128), 0) // HD
+    col = lax.broadcasted_iota(jnp.int32, (128, 128), 1) // HD
+    return jnp.where(row == col, 1.0, 0.0).astype(BF)
+
+
+def half_of(rows, half):
+    lane = lax.broadcasted_iota(jnp.int32, (rows, 128), 1)
+    return jnp.where((lane < HD) == (half == 0), 1.0, 0.0).astype(BF)
+
+
+def other_half(v):
+    lane = lax.broadcasted_iota(jnp.int32, v.shape, 1)
+    return jnp.where(lane % HD < HD // 2, pltpu.roll(v, 128 - HD // 2, 1), pltpu.roll(v, HD // 2, 1))
+
+
+def first_key(block):
+    return max(0, block * BLOCK - SPAN)
+
+
+def forward_kernel(x_ref, w_ref, cos_ref, sin_ref, gain_ref, start_ref, q_o, k_o, v_o, rq_o, rk_o, y_o, bias, send, recv):
+    index, x = lax.axis_index("fsdp"), lax.axis_index("mp")
+    across = (index, 1 - x)
+    greet((across,))
+    length, cols = q_o.shape
+    ones = head_ones()
+
+    def project(i, _):
+        rows = pl.ds(pl.multiple_of(i * BLOCK, BLOCK), BLOCK)
+        states = x_ref[rows]
+        cos, sin = cos_ref[rows], sin_ref[rows]
+        for j, (out, factor_o, scale) in enumerate(((q_o, rq_o, HD**-0.5), (k_o, rk_o, 1.0))):
+            raw = dot_nn(states, w_ref[j])
+            for c in range(0, cols, 128):
+                part = raw[:, c : c + 128]
+                factor = lax.rsqrt(split_dot(part * part, ones) * (1.0 / HD) + EPS)
+                unit = (part * cos + other_half(part) * sin) * factor
+                out[rows, c : c + 128] = ((gain_ref[:, c : c + 128] * unit).astype(BF).astype(F32) * scale).astype(BF)
+                factor_o[rows, c : c + 128] = factor
+        v_o[rows] = dot_nn(states, w_ref[2]).astype(BF)
+        return 0
+
+    lax.fori_loop(0, length // BLOCK, project, 0)
+    copies = []
+    for block in range(length // BLOCK):
+        low = first_key(block)
+        keys = (block + 1) * BLOCK - low
+        rows = pl.ds(block * BLOCK, BLOCK)
+        span = pl.ds(low, keys)
+        kpos = lax.broadcasted_iota(jnp.int32, (BLOCK, keys), 1) + low
+        qpos = lax.broadcasted_iota(jnp.int32, (BLOCK, keys), 0) + block * BLOCK
+        allowed = (kpos >= start_ref[rows]) & (kpos <= qpos)
+        bias[:, :keys] = jnp.where(allowed, 0.0, NEG_FILL)
+
+        def heads(pair, _):
+            c = pl.ds(pl.multiple_of(pair * 128, 128), 128)
+            q, k, v = q_o[rows, c], k_o[span, c], v_o[span, c]
+            outs = []
+            for half in (0, 1):
+                scores = dot_nt(q * half_of(BLOCK, half), k)
+                probs = jnp.exp(scores + bias[:, :keys]).astype(BF)
+                outs.append(dot_nn(probs, v * half_of(keys, half) + half_of(keys, 1 - half)))
+            lane = lax.broadcasted_iota(jnp.int32, (BLOCK, 128), 1)
+            total = pltpu.roll(jnp.where(lane < HD, outs[1], outs[0]), HD, 1)
+            y_o[x, rows, c] = (jnp.where(lane < HD, outs[0], outs[1]) / total).astype(BF)
+            return 0
+
+        lax.fori_loop(0, cols // 128, heads, 0)
+        copy = remote(y_o.at[x, rows], y_o.at[x, rows], send.at[block], recv.at[block], across)
+        copy.start()
+        copies.append(copy)
+    for copy in copies:
+        copy.wait_send()
+    for block in range(length // BLOCK):
+        there = y_o.at[1 - x, pl.ds(block * BLOCK, BLOCK)]
+        remote(there, there, send.at[block], recv.at[block], across).wait_recv()
+
+
+def attention_forward(states, weights, cos, sin, gain, start):
+    length, cols = states.shape[0], gain.shape[1]
+    vspec = pl.BlockSpec(memory_space=VM)
+    blocks = length // BLOCK
+    low = jax.ShapeDtypeStruct((length, cols), BF)
+    full = jax.ShapeDtypeStruct((length, cols), F32)
+    return pl.pallas_call(
+        forward_kernel,
+        out_shape=(low, low, low, full, full, jax.ShapeDtypeStruct((2, length, cols), BF)),
+        in_specs=[vspec] * 6,
+        out_specs=(vspec,) * 6,
+        scratch_shapes=[
+            VM((BLOCK, BLOCK + SPAN), F32),
+            pltpu.SemaphoreType.DMA((blocks,)),
+            pltpu.SemaphoreType.DMA((blocks,)),
+        ],
+        compiler_params=pltpu.CompilerParams(collective_id=4, has_side_effects=True, vmem_limit_bytes=60 * MIB),
+        name="attention_forward",
+    )(states, weights, cos, sin, gain, start)
+
+
+def backward_kernel(
+    x_ref, w_ref, q_ref, k_ref, v_ref, rq_ref, rk_ref, y_ref, dy_ref, do_ref, dri_ref, cos_ref, sin_ref, gain_ref, start_ref,
+    ig_o, head_o, dw_o, bias, dq_s, dk_s, dv_s, low_s, out_s, in_s, send, recv,
+):
+    index, x = lax.axis_index("fsdp"), lax.axis_index("mp")
+    across = (index, 1 - x)
+    greet((across,))
+    length, cols = q_ref.shape
+    width = x_ref.shape[1]
+    ones = head_ones()
+    dk_s[...] = jnp.zeros_like(dk_s)
+    dv_s[...] = jnp.zeros_like(dv_s)
+    head_o[...] = jnp.zeros_like(head_o)
+    copies = {}
+    for block in reversed(range(length // BLOCK)):
+        low = first_key(block)
+        keys = (block + 1) * BLOCK - low
+        rows = pl.ds(block * BLOCK, BLOCK)
+        span = pl.ds(low, keys)
+        kpos = lax.broadcasted_iota(jnp.int32, (keys, BLOCK), 0) + low
+        qpos = lax.broadcasted_iota(jnp.int32, (keys, BLOCK), 1) + block * BLOCK
+        allowed = (kpos >= start_ref[:, block * BLOCK : (block + 1) * BLOCK]) & (kpos <= qpos)
+        bias[:keys] = jnp.where(allowed, 0.0, NEG_FILL)
+
+        def heads(pair, _):
+            c = pl.ds(pl.multiple_of(pair * 128, 128), 128)
+            q, k, v, dy = q_ref[rows, c], k_ref[span, c], v_ref[span, c], dy_ref[rows, c]
+            prod = dy.astype(F32) * y_ref[x, rows, c].astype(F32)
+            prod_high = prod.astype(BF)
+            prod_low = (prod - prod_high.astype(F32)).astype(BF)
+            dq = jnp.zeros((BLOCK, 128), F32)
+            dk = jnp.zeros((keys, 128), F32)
+            dv = jnp.zeros((keys, 128), F32)
+            for half in (0, 1):
+                mask, row = half_of(BLOCK, half), half_of(8, half)
+                qm, dym, km = q * mask, dy * mask, k * half_of(keys, half)
+                expo = jnp.exp(dot_nt(k, qm) + bias[:keys])
+                probs = expo * (1.0 / jnp.sum(expo, axis=0, keepdims=True))
+                delta = (dot_nt(row, prod_high) + dot_nt(row, prod_low))[0:1]
+                dz = (probs * (dot_nt(v, dym) - delta)).astype(BF)
+                dk = dk + dot_nn(dz, qm)
+                dv = dv + dot_nn(probs.astype(BF), dym)
+                dq = dq + dot_tn(dz, km)
+            dq_s[rows, c] = dq * HD**-0.5
+            dk_s[span, c] = dk_s[span, c] + dk
+            dv_s[span, c] = dv_s[span, c] + dv
+            return 0
+
+        lax.fori_loop(0, cols // 128, heads, 0)
+        cos, sin = cos_ref[rows], sin_ref[rows]
+        for c in range(0, cols, 128):
+            s = slice(c, c + 128)
+            gain = gain_ref[:, s]
+            head = jnp.zeros((BLOCK, 128), F32)
+            for j, (grad_s, low_ref, factor_ref, scale) in enumerate(
+                ((dq_s, q_ref, rq_ref, HD**0.5), (dk_s, k_ref, rk_ref, 1.0))
+            ):
+                grad = grad_s[rows, s]
+                unit = low_ref[rows, s].astype(F32) * (scale / gain)
+                head = head + grad * unit
+                grad = grad * gain
+                turned = factor_ref[rows, s] * (grad - unit * (split_dot(grad * unit, ones) * (1.0 / HD)))
+                low_s[j, rows, s] = (turned * cos - other_half(turned) * sin).astype(BF)
+            head_o[:, s] = head_o[:, s] + jnp.sum(head, axis=0, keepdims=True)
+            low_s[2, rows, s] = dv_s[rows, s].astype(BF)
+        for c in range(0, width, 512):
+            part = sum(dot_nt(low_s[j, rows], w_ref[j, c : c + 512]) for j in range(3))
+            out_s[rows, c : c + 512] = part.astype(BF)
+        copy = remote(out_s.at[rows], in_s.at[rows], send.at[block], recv.at[block], across)
+        copy.start()
+        copies[block] = copy
+
+    def grads(i, _):
+        d = pl.ds(pl.multiple_of(i * BLOCK, BLOCK), BLOCK)
+        for j in range(3):
+            dw_o[j, d] = dot_tn(x_ref[:, d], low_s[j]).astype(BF)
+        dw_o[3, d] = dot_tn(do_ref[:, d], y_ref[x]).astype(BF)
+        return 0
+
+    lax.fori_loop(0, width // BLOCK, grads, 0)
+    for block in reversed(range(length // BLOCK)):
+        copies[block].wait()
+
+        def finish(i, _):
+            r = pl.ds(pl.multiple_of(block * BLOCK + i * 32, 32), 32)
+            ig_o[r] = dri_ref[r] + (out_s[r].astype(F32) + in_s[r].astype(F32))
+            return 0
+
+        lax.fori_loop(0, BLOCK // 32, finish, 0)
+
+
+def attention_backward(states, weights, q, k, v, rq, rk, y, dy, do, dri, cos, sin, gain, start):
+    length, width = states.shape
+    cols = gain.shape[1]
+    vspec = pl.BlockSpec(memory_space=VM)
+    blocks = length // BLOCK
+    return pl.pallas_call(
+        backward_kernel,
+        out_shape=(
+            jax.ShapeDtypeStruct((length, width), F32),
+            jax.ShapeDtypeStruct((1, cols), F32),
+            jax.ShapeDtypeStruct((4, width, cols), BF),
+        ),
+        in_specs=[vspec] * 15,
+        out_specs=(vspec,) * 3,
+        scratch_shapes=[
+            VM((BLOCK + SPAN, BLOCK), F32),
+            VM((length, cols), F32),
+            VM((length, cols), F32),
+            VM((length, cols), F32),
+            VM((3, length, cols), BF),
+            VM((length, width), BF),
+            VM((length, width), BF),
+            pltpu.SemaphoreType.DMA((blocks,)),
+            pltpu.SemaphoreType.DMA((blocks,)),
+        ],
+        compiler_params=pltpu.CompilerParams(collective_id=5, has_side_effects=True, vmem_limit_bytes=60 * MIB),
+        name="attention_backward",
+    )(states, weights, q, k, v, rq, rk, y, dy, do, dri, cos, sin, gain, start)
+
+
+ROWS_STEP = 32
+UNIT_STEP = 512
+
+
+def row_factor(v):
+    return lax.rsqrt(jnp.mean(v * v, axis=-1, keepdims=True) + EPS)
+
+
+def unit_back(factor, unit, grad):
+    return factor * (grad - unit * jnp.mean(grad * unit, axis=-1, keepdims=True))
+
+
+def fold(v):
+    return jnp.sum(v.reshape(v.shape[0] // 8, 8, v.shape[1]), axis=0)
+
+
+def feed_kernel(
+    x_ref, y_ref, og_ref, mix_ref, us_ref, wo_own, wo_peer, w_ref,
+    out_o, dri_o, do_o, dy_o, mix_o, us_o, dwu_o, dwg_o, dwd_o,
+    wo_s, wu_s, wg_s, wd_s, o_s, hb_s, u_s, g_s, hid_s, dm_s, dh_s, own_s, got_m, got_d, hout_s,
+    load, store, send_m, recv_m, send_d, recv_d,
+):
+    index, x = lax.axis_index("fsdp"), lax.axis_index("mp")
+    across = (index, 1 - x)
+    length, width = x_ref.shape
+    cols, units = wo_own.shape[2], us_ref.shape[1]
+    loads = [
+        pltpu.make_async_copy(wo_own.at[3], wo_s.at[x], load.at[0]),
+        pltpu.make_async_copy(wo_peer, wo_s.at[1 - x], load.at[1]),
+        pltpu.make_async_copy(w_ref.at[0], wu_s, load.at[2]),
+        pltpu.make_async_copy(w_ref.at[1], wg_s, load.at[3]),
+        pltpu.make_async_copy(w_ref.at[2], wd_s, load.at[4]),
+    ]
+    for copy in loads:
+        copy.start()
+    greet((across,))
+    blocks = length // BLOCK
+    copies_m, copies_d = [], []
+
+    def first_half(r):
+        states = x_ref[r].astype(F32)
+        o = o_s[r]
+        ro = row_factor(o)
+        uo = o * ro
+        mix = mix_ref[0:1]
+        r1 = states + mix * (uo - states)
+        rr = row_factor(r1)
+        return states, ro, uo, rr, r1 * rr
+
+    def by_rows(block, body, init):
+        def run(i, carry):
+            return body(pl.ds(pl.multiple_of(block * BLOCK + i * ROWS_STEP, ROWS_STEP), ROWS_STEP), i, carry)
+
+        return lax.fori_loop(0, BLOCK // ROWS_STEP, run, init)
+
+    def by_cols(total, step, body):
+        def run(i, _):
+            body(pl.ds(pl.multiple_of(i * step, step), step))
+            return 0
+
+        lax.fori_loop(0, total // step, run, 0)
+
+    for block in range(blocks):
+        rows = pl.ds(block * BLOCK, BLOCK)
+        if block == 0:
+            loads[0].wait()
+            loads[1].wait()
+
+        def out_proj(c):
+            o_s[rows, c] = dot_nt(y_ref[0, rows], wo_s[0, c]) + dot_nt(y_ref[1, rows], wo_s[1, c])
+
+        by_cols(width, 512, out_proj)
+
+        def hidden(r, i, _):
+            hb_s[r] = first_half(r)[4].astype(BF)
+            return 0
+
+        by_rows(block, hidden, 0)
+        if block == 0:
+            loads[2].wait()
+            loads[3].wait()
+
+        def gate(f):
+            up = dot_nn(hb_s[rows], wu_s[:, f])
+            gt = dot_nn(hb_s[rows], wg_s[:, f])
+            arg = us_ref[1:2, f] * gt * D**-0.5
+            sig = 1.0 / (1.0 + jnp.exp(-arg))
+            u_s[rows, f] = up.astype(BF)
+            g_s[rows, f] = gt.astype(BF)
+            hid_s[rows, f] = (us_ref[0:1, f] * up * (arg * sig)).astype(BF)
+
+        by_cols(units, UNIT_STEP, gate)
+        if block == 0:
+            loads[4].wait()
+
+        def down(c):
+            own_s[rows, c] = dot_nt(hid_s[rows], wd_s[c]).astype(BF)
+
+        by_cols(width, 512, down)
+        copy = remote(own_s.at[rows], got_m.at[rows], send_m.at[block], recv_m.at[block], across)
+        copy.start()
+        copies_m.append(copy)
+
+    mix_m = jnp.zeros((8, width), F32)
+    us_o[...] = jnp.zeros_like(us_o)
+    outs = []
+    for block in range(blocks):
+        rows = pl.ds(block * BLOCK, BLOCK)
+        copies_m[block].wait()
+        if block >= 2:
+            outs[block - 2].wait()
+
+        def middle(r, i, total):
+            h1 = first_half(r)[4]
+            m = own_s[r].astype(F32) + got_m[r].astype(F32)
+            rm = row_factor(m)
+            um = m * rm
+            mix = mix_ref[1:2]
+            r2 = h1 + mix * (um - h1)
+            rr = row_factor(r2)
+            out = r2 * rr
+            hout_s[block % 2, pl.ds(pl.multiple_of(i * ROWS_STEP, ROWS_STEP), ROWS_STEP)] = out
+            dr2 = unit_back(rr, out, og_ref[r].astype(F32))
+            dm_s[r] = unit_back(rm, um, mix * dr2).astype(BF)
+            dh_s[r] = dr2 * (1.0 - mix)
+            return total + fold(dr2 * (um - h1))
+
+        mix_m = by_rows(block, middle, mix_m)
+        copy = pltpu.make_async_copy(hout_s.at[block % 2], out_o.at[rows], store.at[block])
+        copy.start()
+        outs.append(copy)
+
+        def gate_back(f):
+            dhid = dot_nn(dm_s[rows], wd_s[:, f])
+            up, gt = u_s[rows, f].astype(F32), g_s[rows, f].astype(F32)
+            su, sv = us_ref[0:1, f], us_ref[1:2, f]
+            arg = sv * gt * D**-0.5
+            sig = 1.0 / (1.0 + jnp.exp(-arg))
+            act = dhid * (arg * sig)
+            darg = dhid * su * up * sig * (1.0 + arg * (1.0 - sig))
+            us_o[0:1, f] = us_o[0:1, f] + jnp.sum(act * up, axis=0, keepdims=True)
+            us_o[1:2, f] = us_o[1:2, f] + jnp.sum(darg * gt, axis=0, keepdims=True) * D**-0.5
+            u_s[rows, f] = (act * su).astype(BF)
+            g_s[rows, f] = (darg * sv * D**-0.5).astype(BF)
+
+        by_cols(units, UNIT_STEP, gate_back)
+
+        def up_back(c):
+            own_s[rows, c] = (dot_nt(u_s[rows], wu_s[c]) + dot_nt(g_s[rows], wg_s[c])).astype(BF)
+
+        by_cols(width, 512, up_back)
+        copy = remote(own_s.at[rows], got_d.at[rows], send_d.at[block], recv_d.at[block], across)
+        copy.start()
+        copies_d.append(copy)
+
+    def grads(d):
+        for u in range(0, units, 1024):
+            f = pl.ds(u, 1024)
+            wu_s[d, f] = dot_tn(hb_s[:, d], u_s[:, f]).astype(BF)
+            wg_s[d, f] = dot_tn(hb_s[:, d], g_s[:, f]).astype(BF)
+            wd_s[d, f] = dot_tn(dm_s[:, d], hid_s[:, f]).astype(BF)
+
+    by_cols(width, BLOCK, grads)
+    saves = [
+        pltpu.make_async_copy(src, dst, load.at[j])
+        for j, (src, dst) in enumerate(((wu_s, dwu_o), (wg_s, dwg_o), (wd_s, dwd_o)))
+    ]
+    for copy in saves:
+        copy.start()
+
+    mix_a = jnp.zeros((8, width), F32)
+    for block in range(blocks):
+        rows = pl.ds(block * BLOCK, BLOCK)
+        copies_d[block].wait()
+
+        def last(r, i, total):
+            states, ro, uo, rr, h1 = first_half(r)
+            mix = mix_ref[0:1]
+            dr1 = unit_back(rr, h1, dh_s[r] + (own_s[r].astype(F32) + got_d[r].astype(F32)))
+            dh_s[r] = dr1 * (1.0 - mix)
+            dm_s[r] = unit_back(ro, uo, mix * dr1).astype(BF)
+            return total + fold(dr1 * (uo - states))
+
+        mix_a = by_rows(block, last, mix_a)
+        dy_o[rows] = dot_nn(dm_s[rows], wo_s[x]).astype(BF)
+    ends = [
+        pltpu.make_async_copy(dh_s, dri_o, load.at[3]),
+        pltpu.make_async_copy(dm_s, do_o, load.at[4]),
+    ]
+    for copy in ends:
+        copy.start()
+    mix_o[0:1] = jnp.sum(mix_a, axis=0, keepdims=True)
+    mix_o[1:2] = jnp.sum(mix_m, axis=0, keepdims=True)
+    for copy in outs[-2:] + saves + ends:
+        copy.wait()
+
+
+def feed_forward(states, y, out_grad, mix, scales, attn_full, wo_peer, mlp_full):
+    length, width = states.shape
+    cols, units = y.shape[2], scales.shape[1]
+    vspec, anyspec = pl.BlockSpec(memory_space=VM), pl.BlockSpec(memory_space=pl.ANY)
+    blocks = length // BLOCK
+    sem = pltpu.SemaphoreType.DMA
+
+    def low(*shape):
+        return jax.ShapeDtypeStruct(shape, BF)
+
+    def full(*shape):
+        return jax.ShapeDtypeStruct(shape, F32)
+
+    return pl.pallas_call(
+        feed_kernel,
+        out_shape=(
+            full(length, width), full(length, width), low(length, width), low(length, cols),
+            full(2, width), full(2, units), low(width, units), low(width, units), low(width, units),
+        ),
+        in_specs=[vspec] * 5 + [anyspec] * 3,
+        out_specs=(anyspec, anyspec, anyspec, vspec, vspec, vspec, anyspec, anyspec, anyspec),
+        scratch_shapes=[
+            VM((2, width, cols), BF),
+            VM((width, units), BF), VM((width, units), BF), VM((width, units), BF),
+            VM((length, width), F32), VM((length, width), BF),
+            VM((length, units), BF), VM((length, units), BF), VM((length, units), BF),
+            VM((length, width), BF), VM((length, width), F32),
+            VM((length, width), BF), VM((length, width), BF), VM((length, width), BF),
+            VM((2, BLOCK, width), F32),
+            sem((5,)), sem((blocks,)), sem((blocks,)), sem((blocks,)), sem((blocks,)), sem((blocks,)),
+        ],
+        compiler_params=pltpu.CompilerParams(collective_id=6, has_side_effects=True, vmem_limit_bytes=63 * MIB),
+        name="feed_forward",
+    )(states, y, out_grad, mix, scales, attn_full, wo_peer, mlp_full)
+
+
+def rotary_rows(doc_row, lanes):
+    length = doc_row.shape[0]
+    start = jnp.sum((doc_row[None, :] < doc_row[:, None]).astype(jnp.int32), axis=1)
+    offset = (jnp.arange(length, dtype=jnp.int32) - start).astype(F32)
+    freq = THETA ** (-2.0 * jnp.arange(HD // 2, dtype=F32) / HD)
+    angle = offset[:, None] * freq[None, :]
+    cos, sin = jnp.cos(angle), jnp.sin(angle)
+    repeat = lanes // HD
+    return start, jnp.tile(jnp.concatenate([cos, cos], 1), (1, repeat)), jnp.tile(jnp.concatenate([-sin, sin], 1), (1, repeat))
+
+
+def local_fast(
+    inputs, doc_ids, out_grad, attn_w, attn_mom, attn_avg, mlp_w, mlp_mom, mlp_avg,
+    head_scale, head_mom, mix_rates, mix_mom, unit_scales, unit_mom,
+):
+    fsdp = lax.axis_size("fsdp")
+    tokens = inputs.shape[0] * fsdp * inputs.shape[1]
+    root_tokens = math.sqrt(tokens)
+    width = inputs.shape[2]
+    states = inputs[0]
+    start, cos, sin = rotary_rows(doc_ids[0], 128)
+    gain = head_scale[None]
+    attn_full, mlp_full, wo_peer = gather_weights(attn_w.astype(BF), mlp_w.astype(BF), fsdp)
+    q, k, v, rq, rk, y = attention_forward(states, attn_full, cos, sin, gain, start[:, None])
+    result, dri, do, dy, grad_mix, grad_units, dwu, dwg, dwd = feed_forward(
+        states, y, out_grad[0], mix_rates, unit_scales, attn_full, wo_peer, mlp_full
+    )
+    input_grad, grad_head, dwa = attention_backward(
+        states, attn_full, q, k, v, rq, rk, y, dy, do, dri, cos, sin, gain, start[None]
+    )
+    grad_head = grad_head[0]
+    grad_attn, grad_mlp = scatter_grads(dwa, dwu, dwg, dwd, fsdp)
+    small = jnp.concatenate(
+        [
+            jnp.pad(grad_head, (0, D - grad_head.shape[0])),
+            grad_mix.reshape(-1),
+            grad_units.reshape(-1),
+            jnp.zeros((D,), F32),
+        ]
+    ).reshape(8, D)
+    attn_mom_new, attn_new, attn_avg_new, mlp_mom_new, mlp_new, mlp_avg_new, small = update(
+        grad_attn, grad_mlp, small, attn_w, attn_mom, attn_avg, mlp_w, mlp_mom, mlp_avg,
+        RATE_WEIGHT / root_tokens, width, fsdp,
+    )
+    grad_head, grad_mix, grad_units = small[0, : grad_head.shape[0]], small[1:3], small[3:7].reshape(2, -1)
+    head_mom_new, head_new = nesterov(head_scale, head_mom, grad_head, RATE_HEAD / root_tokens)
+    mix_mom_new, mix_new = nesterov(mix_rates, mix_mom, grad_mix, RATE_MIX / root_tokens)
+    units_mom_new, units_new = nesterov(unit_scales, unit_mom, grad_units, RATE_UNITS / root_tokens)
+    return (
+        result[None], input_grad[None], attn_mom_new, attn_new, attn_avg_new, mlp_mom_new, mlp_new, mlp_avg_new,
+        head_mom_new, head_new, mix_mom_new, mix_new, units_mom_new, units_new,
+    )
+
+
 def local(
     inputs,
     doc_ids,
@@ -702,197 +1213,6 @@
     )
 
 
-def local_fast(
-    inputs,
-    doc_ids,
-    out_grad,
-    attn_w,
-    attn_mom,
-    attn_avg,
-    mlp_w,
-    mlp_mom,
-    mlp_avg,
-    head_scale,
-    head_mom,
-    mix_rates,
-    mix_mom,
-    unit_scales,
-    unit_mom,
-):
-    length = inputs.shape[1]
-    model_width = inputs.shape[2]
-    head_count = head_scale.shape[0] // HD
-    block_rows = min(512, length)
-    block_count = length // block_rows
-    tokens = inputs.shape[0] * lax.axis_size("fsdp") * length
-    doc_row = doc_ids[0]
-    input_low = inputs[0]
-    resid_in = input_low.astype(jnp.float32)
-    cos_table, sin_table = rotary_tables(doc_row)
-    position = jnp.arange(length, dtype=jnp.int32)
-    fsdp = lax.axis_size("fsdp")
-    attn_full, mlp_full, _ = gather_weights(attn_w.astype(BF), mlp_w.astype(BF), fsdp)
-    attn_back, mlp_back = attn_full, mlp_full
-    projected = jnp.einsum(
-        "sd,jdc->jsc", input_low, attn_full[:3], preferred_element_type=jnp.float32
-    )
-    head_gain = head_scale.reshape(head_count, HD)
-    q_rot = rotate(projected[0].reshape(length, head_count, HD), cos_table, sin_table)
-    k_rot = rotate(projected[1].reshape(length, head_count, HD), cos_table, sin_table)
-    q_unit = rms_unit(q_rot)
-    k_unit = rms_unit(k_rot)
-    query_low = (head_gain * q_unit).astype(jnp.bfloat16)
-    key_low = (head_gain * k_unit).astype(jnp.bfloat16)
-    value_low = projected[2].reshape(length, head_count, HD).astype(jnp.bfloat16)
-
-    def scores_of(row_first):
-        query_blk = lax.dynamic_slice_in_dim(query_low, row_first, block_rows, 0)
-        raw_scores = jnp.einsum(
-            "qhe,khe->hqk", query_blk, key_low, preferred_element_type=jnp.float32
-        )
-        row_pos = lax.dynamic_slice_in_dim(position, row_first, block_rows, 0)
-        row_docs = lax.dynamic_slice_in_dim(doc_row, row_first, block_rows, 0)
-        allowed = (row_docs[:, None] == doc_row[None, :]) & (position[None, :] <= row_pos[:, None])
-        return (jnp.where(allowed[None], raw_scores * HD ** (-0.5), NEG_FILL), query_blk)
-
-    def attend(accums, blk_index):
-        scores, query_blk = scores_of(blk_index * block_rows)
-        peak_val = jnp.max(scores, axis=-1, keepdims=True)
-        expo_vals = jnp.exp(scores - peak_val)
-        row_total = jnp.sum(expo_vals, axis=-1, keepdims=True)
-        probs_low = (expo_vals / row_total).astype(jnp.bfloat16)
-        blk_out = jnp.einsum(
-            "hqk,khe->qhe", probs_low, value_low, preferred_element_type=jnp.float32
-        )
-        return (accums, (blk_out, (peak_val + jnp.log(row_total))[..., 0]))
-
-    _, (mixed_blocks, log_totals) = lax.scan(attend, None, jnp.arange(block_count))
-    mixed_low = mixed_blocks.reshape(length, head_count * HD).astype(jnp.bfloat16)
-    attn_part = jnp.einsum("sc,dc->sd", mixed_low, attn_full[3], preferred_element_type=jnp.float32)
-    attn_out = lax.psum(attn_part, "mp")
-    attn_unit = rms_unit(attn_out)
-    resid_one = resid_in + mix_rates[0] * (attn_unit - resid_in)
-    hidden_one = rms_unit(resid_one)
-    hidden_low = hidden_one.astype(jnp.bfloat16)
-    gates = jnp.einsum("sd,jdf->jsf", hidden_low, mlp_full[:2], preferred_element_type=jnp.float32)
-    up_proj = gates[0]
-    gate_proj = gates[1]
-    gate_arg = unit_scales[1] * gate_proj * D ** (-0.5)
-    gate_sig = jax.nn.sigmoid(gate_arg)
-    gate_act = gate_arg * gate_sig
-    units_low = (unit_scales[0] * up_proj * gate_act).astype(jnp.bfloat16)
-    mlp_part = jnp.einsum("sf,df->sd", units_low, mlp_full[2], preferred_element_type=jnp.float32)
-    mlp_out = lax.psum(mlp_part, "mp")
-    mlp_unit = rms_unit(mlp_out)
-    resid_two = hidden_one + mix_rates[1] * (mlp_unit - hidden_one)
-    result = rms_unit(resid_two)
-    cotangent = out_grad[0].astype(jnp.float32)
-    d_resid_two = rms_back(resid_two, cotangent)
-    grad_mix_mlp = jnp.sum(d_resid_two * (mlp_unit - hidden_one), axis=0)
-    d_hidden_one = d_resid_two * (1.0 - mix_rates[1])
-    d_mlp_low = rms_back(mlp_out, mix_rates[1] * d_resid_two).astype(jnp.bfloat16)
-    d_units = jnp.einsum("sd,df->sf", d_mlp_low, mlp_back[2], preferred_element_type=jnp.float32)
-    d_up = d_units * unit_scales[0] * gate_act
-    d_arg = d_units * unit_scales[0] * up_proj * gate_sig * (1.0 + gate_arg * (1.0 - gate_sig))
-    d_gate = d_arg * unit_scales[1] * D ** (-0.5)
-    grad_units = jnp.stack(
-        [
-            jnp.sum(d_units * up_proj * gate_act, axis=0),
-            jnp.sum(d_arg * gate_proj * D ** (-0.5), axis=0),
-        ]
-    )
-    d_gates_low = jnp.stack([d_up, d_gate]).astype(jnp.bfloat16)
-    mlp_back_part = jnp.einsum(
-        "jsf,jdf->sd", d_gates_low, mlp_back[:2], preferred_element_type=jnp.float32
-    )
-    d_hidden_one = d_hidden_one + lax.psum(mlp_back_part, "mp")
-    w_u = jnp.einsum("sd,sf->df", hidden_low, d_gates_low[0], preferred_element_type=jnp.float32).astype(BF)
-    w_g = jnp.einsum("sd,sf->df", hidden_low, d_gates_low[1], preferred_element_type=jnp.float32).astype(BF)
-    w_d = jnp.einsum("sd,sf->df", d_mlp_low, units_low, preferred_element_type=jnp.float32).astype(BF)
-    d_resid_one = rms_back(resid_one, d_hidden_one)
-    grad_mix_attn = jnp.sum(d_resid_one * (attn_unit - resid_in), axis=0)
-    d_resid_in = d_resid_one * (1.0 - mix_rates[0])
-    d_attn_low = rms_back(attn_out, mix_rates[0] * d_resid_one).astype(jnp.bfloat16)
-    d_mixed = jnp.einsum("sd,dc->sc", d_attn_low, attn_back[3], preferred_element_type=jnp.float32)
-    d_mixed = d_mixed.astype(jnp.bfloat16).reshape(length, head_count, HD)
-
-    def attend_back(accums, blk_index):
-        d_key, d_value = accums
-        row_first = blk_index * block_rows
-        scores, query_blk = scores_of(row_first)
-        blk_total = lax.dynamic_index_in_dim(log_totals, blk_index, 0, keepdims=False)
-        attn_probs = jnp.exp(scores - blk_total[..., None])
-        d_out_blk = lax.dynamic_slice_in_dim(d_mixed, row_first, block_rows, 0)
-        d_probs = jnp.einsum(
-            "qhe,khe->hqk", d_out_blk, value_low, preferred_element_type=jnp.float32
-        )
-        d_scores = attn_probs * (d_probs - jnp.sum(attn_probs * d_probs, axis=-1, keepdims=True))
-        d_raw_low = (d_scores * HD ** (-0.5)).astype(jnp.bfloat16)
-        d_query = jnp.einsum("hqk,khe->qhe", d_raw_low, key_low, preferred_element_type=jnp.float32)
-        d_key = d_key + jnp.einsum(
-            "hqk,qhe->khe", d_raw_low, query_blk, preferred_element_type=jnp.float32
-        )
-        d_value = d_value + jnp.einsum(
-            "hqk,qhe->khe",
-            attn_probs.astype(jnp.bfloat16),
-            d_out_blk,
-            preferred_element_type=jnp.float32,
-        )
-        return ((d_key, d_value), d_query)
-
-    zero_heads = jnp.zeros((length, head_count, HD), jnp.float32)
-    (d_key_all, d_value_all), d_query_blocks = lax.scan(
-        attend_back, (zero_heads, zero_heads), jnp.arange(block_count)
-    )
-    d_query_all = d_query_blocks.reshape(length, head_count, HD)
-    grad_head = jnp.sum(d_query_all * q_unit + d_key_all * k_unit, axis=0).reshape(-1)
-    d_query_raw = rotate_back(rms_back(q_rot, head_gain * d_query_all), cos_table, sin_table)
-    d_key_raw = rotate_back(rms_back(k_rot, head_gain * d_key_all), cos_table, sin_table)
-    d_proj_low = jnp.stack(
-        [
-            d_query_raw.reshape(length, -1),
-            d_key_raw.reshape(length, -1),
-            d_value_all.reshape(length, -1),
-        ]
-    ).astype(jnp.bfloat16)
-    grad_mix = jnp.stack([grad_mix_attn, grad_mix_mlp])
-    attn_back_part = jnp.einsum(
-        "jsc,jdc->sd", d_proj_low, attn_back[:3], preferred_element_type=jnp.float32
-    )
-    input_grad = d_resid_in + lax.psum(attn_back_part.astype(jnp.bfloat16), "mp").astype(
-        jnp.float32
-    )
-    in_terms = jnp.einsum("sd,jsc->jdc", input_low, d_proj_low, preferred_element_type=jnp.float32)
-    out_terms = jnp.einsum("sd,sc->dc", d_attn_low, mixed_low, preferred_element_type=jnp.float32)
-    w_a = jnp.concatenate([in_terms, out_terms[None]], 0).astype(BF)
-    grad_attn, grad_mlp = scatter_grads(w_a, w_u, w_g, w_d, fsdp)
-    root_tokens = math.sqrt(tokens)
-    weight_rate = RATE_WEIGHT / root_tokens
-    small = jnp.concatenate([jnp.pad(grad_head, (0, D - grad_head.shape[0])), grad_mix.reshape(-1), grad_units.reshape(-1), jnp.zeros((D,), F32)]).reshape(8, D)
-    attn_mom_new, attn_new, attn_avg_new, mlp_mom_new, mlp_new, mlp_avg_new, small = update(
-        grad_attn, grad_mlp, small, attn_w, attn_mom, attn_avg, mlp_w, mlp_mom, mlp_avg, weight_rate, model_width, fsdp)
-    grad_head, grad_mix, grad_units = small[0, : grad_head.shape[0]], small[1:3], small[3:7].reshape(2, -1)
-    head_mom_new, head_new = nesterov(head_scale, head_mom, grad_head, RATE_HEAD / root_tokens)
-    mix_mom_new, mix_new = nesterov(mix_rates, mix_mom, grad_mix, RATE_MIX / root_tokens)
-    units_mom_new, units_new = nesterov(unit_scales, unit_mom, grad_units, RATE_UNITS / root_tokens)
-    return (
-        result[None],
-        input_grad[None],
-        attn_mom_new,
-        attn_new,
-        attn_avg_new,
-        mlp_mom_new,
-        mlp_new,
-        mlp_avg_new,
-        head_mom_new,
-        head_new,
-        mix_mom_new,
-        mix_new,
-        units_mom_new,
-        units_new,
-    )
-
-
 def solution(mesh):
     fast = D // mesh.shape["fsdp"] % 16 == 0 and mesh.shape["fsdp"] % 8 == 0
     placed = (

time: 989 us -> 471 us (0.48)
  waiting for transfers between devices: 280 us -> 0 us
  matrix products: 279 us -> 0 us
  Pallas kernels: 223 us -> 441 us
  local copies, waits for them, and re-layouts: 94.4 us -> 18.9 us
  other arithmetic: 80.4 us -> 6.84 us
  between operations: 15.1 us -> 1.09 us
    psum x4 -> x0, waiting for transfers between devices: 280 us -> none  [the longest x1 107 us: local_fast(): attn_out = lax.psum(attn_part, 'mp')]
    dot_general x27 -> x0, matrix products: 279 us -> none  [the longest x2 50.8 us: attend_back(): jnp.einsum('hqk,khe->qhe', d_raw_low, key_low, preferred_element_type=jnp...]
    pallas_call x0 -> x3, Pallas kernels: none -> 220 us  [the longest x1 111 us: feed_forward(): pl.pallas_call(feed_kernel, out_shape=(full(length, width), full(length,...]
    reduce_sum x13 -> x1, other arithmetic: 45.5 us -> 1.32 us  [rotary_rows(): jnp.sum((doc_row[None, :] < doc_row[:, None]).astype(jnp.int32), axis=1)]
    dynamic_update_slice x4 -> x0, local copies, waits for them, and re-layouts: 43.6 us -> none  [local_fast(): lax.scan(attend, None, jnp.arange(block_count))]
    unnamed x164 -> x46, local copies, waits for them, and re-layouts: 20.9 us -> 13.7 us
  transfers between devices with their start and end apart: 4 -> 0, of which waited for: 3 -> 0; matrix products, arithmetic and copies ran while one was open for 7% -> 0% of each run, Pallas kernels for 12% -> 0%
where the time goes in v2:
time: 471 us; the launch traced here: 468 us
  Pallas kernels  441 us (94%)
  local copies, waits for them, and re-layouts  18.9 us (4%)
  other arithmetic  6.84 us (1%)
    pallas_call x1, Pallas kernels, feed_forward(): pl.pallas_call(feed_kernel, out_shape=(full(length, width), full(length,...  111 us
    pallas_call x1, Pallas kernels, gather_weights(): pl.pallas_call(functools.partial(gather_kernel, chips), out_shape=(jax.Sh...  104 us
    pallas_call x1, Pallas kernels, scatter_grads(): pl.pallas_call(functools.partial(scatter_kernel, chips), out_shape=(jax.S...  95.8 us
    pallas_call x1, Pallas kernels, attention_backward(): pl.pallas_call(backward_kernel, out_shape=(jax.ShapeDtypeStruct((length,...  67.1 us
    pallas_call x1, Pallas kernels, attention_forward(): pl.pallas_call(forward_kernel, out_shape=(low, low, low, full, full, jax....  41.8 us
    pallas_call x1, Pallas kernels, update(): pl.pallas_call(functools.partial(update_kernel, stages, rate, width), out...  21.3 us
    unnamed x46, local copies, waits for them, and re-layouts  13.7 us

profile of v2, /device:TPU:0, one launch (start us, length us, event | category | flops | bytes accessed | tf_op | source)
XLA Modules:
  0.0 467.8 jit_solution(17084992743331136098)
XLA Ops:
  0.6 1.3 convert_reduce_fusion
  2.7 1.0 copy.34.cos_ref
  3.7 1.0 copy.35.sin_ref
  4.7 1.0 convert_element_type.19.mlp_ref
  5.7 0.7 convert_element_type.18.attn_ref
  6.4 104.2 %gather_weights.1 = (bf16[4,1024,512]{2,1,0:T(8,128)(2,1)}, bf16[3,1024,2048]{2,1,0:T(8,128)(2,1)}, bf16[1024,512]{1,0:T(8,128)(2,1)}) custom-call(bf16[4,64,512]{2,1,0:T(8,128)(2,1)} %convert_element_type.18.attn_ref, bf16[3,64,2048]{2,1,0:T(8,128)(2,1)} %convert_element_type.19.mlp_ref), custom_call_target="tpu_custom_call" | custom-call | tf_op jit(solution)/shard_map/gather_weights/pallas_call | solution.py:247
  110.6 1.0 copy.36.start_ref
  111.6 41.8 %attention_forward.1 = (bf16[1024,512]{1,0:T(8,128)(2,1)}, bf16[1024,512]{1,0:T(8,128)(2,1)}, bf16[1024,512]{1,0:T(8,128)(2,1)}, f32[1024,512]{1,0:T(8,128)}, f3...) custom-call(bf16[1024,1024]{1,0:T(8,128)(2,1)} %bitcast.22, bf16[4,1024,512]{2,1,0:T(8,128)(2,1)} %get-tuple-element.44.w_ref.wo_own, ...), custom_call_target="tpu_custom_call" | custom-call | tf_op jit(solution)/shard_map/attention_forward/pallas_call | solution.py:570
  153.4 110.8 %feed_forward.1 = (f32[1024,1024]{1,0:T(8,128)}, f32[1024,1024]{1,0:T(8,128)}, bf16[1024,1024]{1,0:T(8,128)(2,1)}, bf16[1024,512]{1,0:T(8,128)(2,1)}, f32[2,1024...) custom-call(bf16[1024,1024]{1,0:T(8,128)(2,1)} %bitcast.23, ...), custom_call_target="tpu_custom_call" | custom-call | tf_op jit(solution)/shard_map/feed_forward/pallas_call | solution.py:916
  264.2 67.1 %attention_backward.1 = (f32[1024,1024]{1,0:T(8,128)}, f32[1,512]{1,0:T(1,128)}, bf16[4,1024,512]{2,1,0:T(8,128)(2,1)}) custom-call(bf16[1024,1024]{1,0:T(8,128)(2,1)} %bitcast.24, bf16[4,1024,512]{2,1,0:T(8,128)(2,1)} %get-tuple-element.44.w_ref.wo_own, bf16[1024,512]{1,0:T(8,128)(2,1)} %get-tuple-element.49.q_ref, ...), custom_call_target="tpu_custom_call" | custom-call | tf_op jit(solution)/shard_map/attention_backward/pallas_call | solution.py:681
  332.7 95.8 %scatter_grads.1 = (f32[4,64,512]{2,1,0:T(8,128)}, f32[3,64,2048]{2,1,0:T(8,128)}) custom-call(bf16[4,16,64,512]{3,2,1,0:T(8,128)(2,1)} %bitcast.30, bf16[16,64,2048]{2,1,0:T(8,128)(2,1)} %bitcast.27, bf16[16,64,2048]{2,1,0:T(8,128)(2,1)} %bitcast.28, bf16[16,64,2048]{2,1,0:T(8,128)(2,1)} %bitcast.29), custom_call_target="tpu_custom_call" | custom-call | tf_op jit(solution)/shard_map/scatter_grads/pallas_call | solution.py:368
  428.6 21.3 %update_weights.1 = (f32[4,64,512]{2,1,0:T(8,128)}, f32[4,64,512]{2,1,0:T(8,128)}, f32[4,64,512]{2,1,0:T(8,128)}, f32[3,64,2048]{2,1,0:T(8,128)}, f32[3,64,2048]...) custom-call(f32[4,64,512]{2,1,0:T(8,128)} %get-tuple-element.62.ga, f32[3,64,2048]{2,1,0:T(8,128)} %get-tuple-element.63.gm, ...), custom_call_target="tpu_custom_call" | custom-call | tf_op jit(solution)/shard_map/update_weights/pallas_call | solution.py:466
  449.9 0.8 slice.11
  451.3 1.4 multiply_subtract_fusion.1
  452.7 0.7 slice.9
  454.0 4.9 %copy.51 = f32[1,1024,1024]{2,1,0:T(8,128)} copy(f32[1,1024,1024]{2,1,0:T(8,128)} %bitcast.25) | data formatting | bytes 8388608
  458.9 2.0 copy.52
  461.0 0.8 copy.53
  461.8 0.8 copy.54
  462.6 0.8 copy.55
  463.4 1.1 copy.56
  464.5 1.1 copy.57
  465.7 0.8 copy-done.3
  466.5 1.1 copy.58
  (49 shorter events, 3.3 us)
Async XLA Ops:
  2.0 108.6 %copy-start.10 = (s32[1024]{0:T(1024)}, s32[1024]{0:T(1024)S(1)}, u32[]{:S(2)}) copy-start(s32[1024]{0:T(1024)S(1)} %convert_reduce_fusion) | copy-start | bytes 12292
  2.6 2.2 copy-start
  3.7 2.0 copy-start.2
  264.2 67.1 %copy-start.14 = (f32[2,2048]{1,0:T(2,128)S(1)}, f32[2,2048]{1,0:T(2,128)}, u32[]{:S(2)}) copy-start(f32[2,2048]{1,0:T(2,128)} %get-tuple-element.66) | copy-start | bytes 49156
  264.2 67.1 %copy-start.16 = (f32[2,1024]{1,0:T(2,128)S(1)}, f32[2,1024]{1,0:T(2,128)}, u32[]{:S(2)}) copy-start(f32[2,1024]{1,0:T(2,128)} %get-tuple-element.65) | copy-start | bytes 24580
  428.5 22.2 %copy-start.9 = (f32[2,2048]{1,0:T(2,128)S(1)}, f32[2,2048]{1,0:T(2,128)}, u32[]{:S(2)}) copy-start(f32[2,2048]{1,0:T(2,128)} %us_ref.1) | copy-start | bytes 49156
  428.5 22.2 %copy-start.13 = (f32[2,2048]{1,0:T(2,128)S(1)}, f32[2,2048]{1,0:T(2,128)}, u32[]{:S(2)}) copy-start(f32[2,2048]{1,0:T(2,128)} %param.29) | copy-start | bytes 49156
  428.5 22.8 %copy-start.11 = (f32[2,1024]{1,0:T(2,128)S(1)}, f32[2,1024]{1,0:T(2,128)}, u32[]{:S(2)}) copy-start(f32[2,1024]{1,0:T(2,128)} %mix_ref.1) | copy-start | bytes 24580
  428.5 22.8 %copy-start.15 = (f32[2,1024]{1,0:T(2,128)S(1)}, f32[2,1024]{1,0:T(2,128)}, u32[]{:S(2)}) copy-start(f32[2,1024]{1,0:T(2,128)} %param.27) | copy-start | bytes 24580
  428.6 24.9 %copy-start.12 = (f32[512]{0:T(512)S(1)}, f32[512]{0:T(512)}, u32[]{:S(2)}) copy-start(f32[512]{0:T(512)} %param.24) | copy-start | bytes 6148
  428.6 24.9 %copy-start.17 = (f32[512]{0:T(512)S(1)}, f32[512]{0:T(512)}, u32[]{:S(2)}) copy-start(f32[512]{0:T(512)} %param.25) | copy-start | bytes 6148
  454.0 4.9 %copy-start.1 = (f32[1024,1024]{1,0:T(8,128)S(1)}, f32[1024,1024]{1,0:T(8,128)}, u32[]{:S(2)}) copy-start(f32[1024,1024]{1,0:T(8,128)} %get-tuple-element.57) | copy-start | bytes 12582916
  458.9 2.0 copy-start.8
  458.9 2.8 copy-start.7
  461.0 1.6 copy-start.6
  461.0 2.4 copy-start.5
  462.6 1.9 copy-start.4
  464.5 2.0 copy-start.3
